TPU v7x, 128 devices: a whole 4x4x4 slice. The times are simulated.
128 devices in a mesh: section: 2 (over x_lo), lat: 16 (over z, y), lon: 4 (over x_hi, core).
Axes of the slice: x: 4 (x_hi: 2, x_lo: 2; x = x_hi * 2 + x_lo), y: 4, z: 4, core: 2. Of those that a mesh axis runs over, the one named last changes fastest.
Arguments:
- state: bfloat16 [2, 112, 360, 1024], P('section', 'lat', 'lon'), may hold values from -6 to 6
- fresh: bfloat16 [112, 360, 1024], P('lat', 'lon'), may hold values from -6 to 6
- cutoff: int32 [3], replicated, may hold values from 0 to 15
- plan: int32 [2, 2], replicated, may hold values from 0 to 1
- lmax: int32 [2], replicated, may hold values from 56 to 112, as said below
- mmax: int32 [2], replicated, may hold values from 24 to 96, as said below
- cutoff_table: float32 [16, 1024], replicated, may hold values from -3 to 3
- norm_gains: float32 [2, 2, 2, 1024], P('section'), may hold values from 0.1 to 1.9
- filters: float32 [2, 2, 2, 112, 1024], P('section', None, None, None, 'lon'), may hold values from -5 to 5
- w_in: bfloat16 [2, 2, 1024, 4096], P('section', None, 'lat'), may hold values from -0.1875 to 0.1875
- w_out: bfloat16 [2, 2, 1024, 4096], P('section', None, 'lat'), may hold values from -0.09375 to 0.09375
Outputs:
- first_pass: bfloat16 [2, 112, 360, 1024], P('section', 'lat', 'lon')
- second_pass: bfloat16 [2, 112, 360, 1024], P('section', 'lat', 'lon')
Inputs may be any that keep to these rules, and one draw needn't show every extreme that they name: `lmax`: some section keeps all 112 degrees in every draw. `mmax`: some section keeps all 96 wavenumbers in every draw.
All inputs are finite; a program needn't handle non-finite values.
Results may differ from a plain program's by a relative error of at most 0.01.
Values may be sent and summed in bfloat16 or wider, within the bound.
A program may use at most 384 MiB of HBM per device.

v0:
```python
import functools
import math

import jax
import jax.numpy as jnp
import numpy as np
from jax import lax
from jax.experimental import pallas as pl
from jax.experimental.pallas import tpu as pltpu
from jax.sharding import PartitionSpec as P

MM = 96
MESH = pl.DeviceIdType.MESH
BF16 = jnp.bfloat16
F32 = jnp.float32
VMEM = 60 * 1024 * 1024
LON_PAD = 96
MODE_PAD = 16
GROUPS = ((0, 4), (4, 3))


def passed_along(value, axis, steps):
    count = lax.axis_size(axis)
    leading, last = (max(0, -steps), min(count, count - steps))
    return lax.ppermute(value, axis, [(source, source + steps) for source in range(leading, last)])


def legendre_table(n_orders, n_rows, n_degrees):
    theta = math.pi * (np.arange(n_rows) + 0.5) / n_rows
    cosine, sine = np.cos(theta), np.sin(theta)
    table = np.zeros((n_degrees, n_orders, n_rows))
    for m in range(n_orders):
        log_start = (
            0.5 * math.log((2.0 * m + 1.0) / (4.0 * math.pi))
            + math.lgamma(m + 0.5) - math.lgamma(0.5) - math.lgamma(m + 1.0)
        )
        table[m, m] = np.exp(log_start + m * np.log(sine))
        for l in range(m + 1, n_degrees):
            coef_a = math.sqrt((4.0 * l * l - 1.0) / (l * l - m * m))
            coef_b = math.sqrt(max((l - 1.0) ** 2 - m * m, 0.0) / max(4.0 * (l - 1.0) ** 2 - 1.0, 1.0))
            before = table[l - 2, m] if l - 2 >= m else 0.0
            table[l, m] = coef_a * (cosine * table[l - 1, m] - coef_b * before)
    quad = 2.0 * math.pi * (math.pi / n_rows) * sine
    return table, table * quad


def spectral_tables(n_lat, n_lon, n_rows, n_cols, n_degrees):
    m_local = MM // n_lat
    all_cols = n_cols * n_lon
    phase = 2.0 * math.pi * ((np.arange(all_cols)[:, None] * np.arange(MM)[None, :]) % all_cols) / all_cols
    weight = np.where(np.arange(MM) == 0, 1.0, 2.0)
    forward = np.zeros((n_lat, MODE_PAD, n_lon, LON_PAD))
    inverse = np.zeros((n_lon, LON_PAD, n_lat, MODE_PAD))
    parts = ((np.cos(phase) / all_cols, weight * np.cos(phase)), (-np.sin(phase) / all_cols, -weight * np.sin(phase)))
    for r, (fwd, inv) in enumerate(parts):
        fwd = fwd.reshape(n_lon, n_cols, n_lat, m_local)
        inv = inv.reshape(n_lon, n_cols, n_lat, m_local)
        forward[:, r * m_local : (r + 1) * m_local, :, :n_cols] = fwd.transpose(2, 3, 0, 1)
        inverse[:, :n_cols, :, r * m_local : (r + 1) * m_local] = inv
    forward = forward.reshape(n_lat * MODE_PAD, n_lon * LON_PAD)
    inverse = inverse.reshape(n_lon * LON_PAD, n_lat * MODE_PAD)
    plain, weighted = legendre_table(MM, n_rows * n_lat, n_degrees)
    split = (n_degrees, n_lat, m_local, n_lat, n_rows)
    weighted = weighted.reshape(split).transpose(1, 2, 0, 3, 4).reshape(n_lat, m_local, n_degrees, n_lat * n_rows)
    padded = np.zeros((n_lat, m_local, n_lat, 8, n_degrees))
    padded[:, :, :, :n_rows] = plain.reshape(split).transpose(1, 2, 3, 4, 0)
    padded = padded.reshape(n_lat, m_local, n_lat * 8, n_degrees)
    return tuple(t.astype(BF16) for t in (forward, inverse, weighted, padded))


def layer_norm(values, gain):
    scale = 1.0 / values.shape[-1]
    center = values - jnp.sum(values, axis=-1, keepdims=True) * scale
    spread = jnp.sum(center * center, axis=-1, keepdims=True) * scale
    return center * lax.rsqrt(spread + 1e-05) * gain


def lon_peer(me, d):
    return lax.rem(me // 2 + d // 2, 2) * 2 + lax.rem(lax.rem(me, 2) + d % 2, 2)


def spec_kernel(
    tick, n_section, plan, cutoff, lmax, mmax, tok, cut_table, gains, filters, fwd, inv, leg_hbm, legt_hbm,
    v_out, own_out, sib_out,
    norm, x_all, spec, y_all, y_f32, f_f32, back, z_all, o_all, r_all, vbuf, nbuf, leg, legt,
    a_send, a_recv, b_send, b_recv, c_send, c_recv, d_send, d_recv, n_send, n_recv, loc,
):
    section, lat, lon = (lax.axis_index(a) for a in ("section", "lat", "lon"))
    n_lat = spec.shape[0]
    n_rows, n_cols, width = tok.shape
    n_degrees, part = filters.shape[3], filters.shape[4]
    m_local = leg.shape[0]
    half = part // 2
    sibling = lon_peer(lon, 1)

    barrier = pltpu.get_barrier_semaphore()
    for d in (1, 2, 3):
        pl.semaphore_signal(barrier, inc=1, device_id={"lon": lon_peer(lon, d)}, device_id_type=MESH)

    def greet(d, carry):
        pl.semaphore_signal(barrier, inc=1, device_id={"lat": lax.rem(lat + d, n_lat)}, device_id_type=MESH)
        return carry

    lax.fori_loop(1, n_lat, greet, 0)
    get_leg = pltpu.make_async_copy(leg_hbm.at[lat], leg, loc.at[0])
    get_legt = pltpu.make_async_copy(legt_hbm.at[lat], legt, loc.at[1])
    get_leg.start()
    get_legt.start()

    block = plan[tick, section]
    cut = cutoff[tick - section + n_section - 1]
    l_max, m_max = lmax[section], mmax[section]
    embed = cut_table[pl.ds(cut, 1), :]
    gain_one = gains[0, block, 0:1, :]
    gain_two = gains[0, block, 1:2, :]
    norm[:, :, LON_PAD - 16 :, :] = jnp.zeros((4, n_rows, 16, part), BF16)
    f_f32[...] = jnp.zeros_like(f_f32)
    pl.semaphore_wait(barrier, 3 + n_lat - 1)

    def send_a(j, d):
        peer = lon_peer(lon, d)
        return pltpu.make_async_remote_copy(
            src_ref=norm.at[peer, j], dst_ref=x_all.at[lon, j], send_sem=a_send.at[d, j],
            recv_sem=a_recv.at[d, j], device_id={"lon": peer}, device_id_type=MESH)

    def take_a(j, d):
        peer = lon_peer(lon, d)
        return pltpu.make_async_remote_copy(
            src_ref=norm.at[peer, j], dst_ref=x_all.at[peer, j], send_sem=a_send.at[d, j],
            recv_sem=a_recv.at[d, j], device_id={"lon": peer}, device_id_type=MESH)

    def first_norm(j, carry):
        base = tok[j].astype(F32) + embed
        out = layer_norm(base, gain_one).astype(BF16)
        for q in range(4):
            norm[q, j, 0:n_cols, :] = out[:, q * part : (q + 1) * part]
        for d in (2, 3, 1):
            send_a(j, d).start()
        x_all[lon, j] = norm[lon, j]
        return carry

    lax.fori_loop(0, n_rows, first_norm, 0)

    def moved(src, dst, send, recv, mine, slot, g, d):
        first, count = GROUPS[g]
        peer = lax.rem(lat + d, n_lat)
        origin = lax.rem(lat - d + n_lat, n_lat)
        where = lat if mine else origin
        return pltpu.make_async_remote_copy(
            src_ref=src.at[peer, pl.ds(first, count)], dst_ref=dst.at[where, pl.ds(first, count)],
            send_sem=send.at[g, d], recv_sem=recv.at[g, d], device_id={"lat": peer}, device_id_type=MESH)

    def zonal(j, carry):
        for d in (1, 2, 3):
            take_a(j, d).wait_recv()
        wide = x_all[:, j].reshape(4 * LON_PAD, part)
        out = jnp.dot(fwd[...], wide, preferred_element_type=F32)
        spec[:, j] = out.astype(BF16).reshape(n_lat, MODE_PAD, part)
        return carry

    for g, (first, count) in enumerate(GROUPS):
        lax.fori_loop(first, first + count, zonal, 0)

        def send_b(d, carry, g=g):
            moved(spec, y_all, b_send, b_recv, True, 0, g, d).start()
            return carry

        lax.fori_loop(1, n_lat, send_b, 0)

    rows = n_rows * MODE_PAD

    def widen(src, value):
        at = pl.multiple_of(src * rows, 16)
        value = value.reshape(rows, part).astype(F32)
        y_f32[0, pl.ds(at, rows), :] = value[:, :half]
        y_f32[1, pl.ds(at, rows), :] = value[:, half:]

    widen(lat, spec[lat])

    def take_b(d, carry):
        for g in range(len(GROUPS)):
            moved(spec, y_all, b_send, b_recv, False, 0, g, d).wait_recv()
        origin = lax.rem(lat - d + n_lat, n_lat)
        widen(origin, y_all[origin])
        return carry

    get_leg.wait()
    get_legt.wait()
    lax.fori_loop(1, n_lat, take_b, 0)

    fil_re = filters[0, block, 0]
    fil_im = filters[0, block, 1]
    degree = lax.broadcasted_iota(jnp.int32, (n_degrees, part), 0)
    n_lines = n_lat * n_rows
    for m in range(m_local):
        pieces = [y_f32[h, pl.ds(r * m_local + m, n_lines, stride=MODE_PAD), :] for r in (0, 1) for h in (0, 1)]
        column = jnp.concatenate(pieces, axis=1).astype(BF16)
        coeff = jnp.dot(leg[m], column, preferred_element_type=F32)
        co_re, co_im = coeff[:, :part], coeff[:, part:]
        order = lat * m_local + m
        keep = (degree < l_max) & (jnp.full((n_degrees, part), order, jnp.int32) < m_max)
        out_re = jnp.where(keep, co_re * fil_re - co_im * fil_im, 0.0)
        out_im = jnp.where(keep, co_re * fil_im + co_im * fil_re, 0.0)
        out = jnp.concatenate([out_re, out_im], axis=1).astype(BF16)
        lines = jnp.dot(legt[m], out, preferred_element_type=F32)
        for r in (0, 1):
            for h in (0, 1):
                at = (2 * r + h) * half
                f_f32[h, pl.ds(r * m_local + m, n_lat * 8, stride=MODE_PAD), :] = lines[:, at : at + half]

    def narrow(peer):
        at = pl.multiple_of(peer * (8 * MODE_PAD), 16)
        value = jnp.concatenate([f_f32[h, pl.ds(at, rows), :] for h in (0, 1)], axis=1)
        return value.astype(BF16).reshape(n_rows, MODE_PAD, part)

    def send_c(d, carry):
        peer = lax.rem(lat + d, n_lat)
        back[peer] = narrow(peer)
        for g in range(len(GROUPS)):
            moved(back, z_all, c_send, c_recv, True, 0, g, d).start()
        return carry

    lax.fori_loop(1, n_lat, send_c, 0)
    z_all[lat] = narrow(lat)

    def send_d(j, d):
        peer = lon_peer(lon, d)
        return pltpu.make_async_remote_copy(
            src_ref=o_all.at[peer, j], dst_ref=r_all.at[lon, j], send_sem=d_send.at[d, j],
            recv_sem=d_recv.at[d, j], device_id={"lon": peer}, device_id_type=MESH)

    def take_d(j, d):
        peer = lon_peer(lon, d)
        return pltpu.make_async_remote_copy(
            src_ref=o_all.at[peer, j], dst_ref=r_all.at[peer, j], send_sem=d_send.at[d, j],
            recv_sem=d_recv.at[d, j], device_id={"lon": peer}, device_id_type=MESH)

    def unzonal(j, carry):
        modes = z_all[:, j].reshape(n_lat * MODE_PAD, part)
        out = jnp.dot(inv[...], modes, preferred_element_type=F32)
        o_all[:, j] = out.astype(BF16).reshape(4, LON_PAD, part)
        for d in (2, 3, 1):
            send_d(j, d).start()
        r_all[lon, j] = o_all[lon, j]
        return carry

    for g, (first, count) in enumerate(GROUPS):

        def take_c(d, carry, g=g):
            moved(back, z_all, c_send, c_recv, False, 0, g, d).wait_recv()
            return carry

        lax.fori_loop(1, n_lat, take_c, 0)
        lax.fori_loop(first, first + count, unzonal, 0)

    def put_v(j):
        return pltpu.make_async_copy(vbuf.at[j], v_out.at[j], loc.at[2 + j])

    def put_own(j):
        return pltpu.make_async_copy(nbuf.at[j], own_out.at[j], loc.at[2 + n_rows + j])

    def put_sib(j):
        return pltpu.make_async_remote_copy(
            src_ref=nbuf.at[j], dst_ref=sib_out.at[j], send_sem=n_send.at[j], recv_sem=n_recv.at[j],
            device_id={"lon": sibling}, device_id_type=MESH)

    def second_norm(j, carry):
        for d in (1, 2, 3):
            take_d(j, d).wait_recv()
        spectral = jnp.concatenate([r_all[q, j, 0:n_cols, :] for q in range(4)], axis=1).astype(F32)
        mixed = tok[j].astype(F32) + embed + spectral
        vbuf[j] = mixed
        nbuf[j, 0:n_cols, :] = layer_norm(mixed, gain_two).astype(BF16)
        put_sib(j).start()
        put_v(j).start()
        put_own(j).start()
        return carry

    nbuf[:, LON_PAD - 16 :, :] = jnp.zeros((n_rows, 16, width), BF16)
    lax.fori_loop(0, n_rows, second_norm, 0)

    def finish_rows(j, carry):
        for d in (1, 2, 3):
            send_a(j, d).wait_send()
            send_d(j, d).wait_send()
        put_v(j).wait()
        put_own(j).wait()
        put_sib(j).wait()
        return carry

    def finish_lat(d, carry):
        for g in range(len(GROUPS)):
            moved(spec, y_all, b_send, b_recv, True, 0, g, d).wait_send()
            moved(back, z_all, c_send, c_recv, True, 0, g, d).wait_send()
        return carry

    lax.fori_loop(1, n_lat, finish_lat, 0)
    lax.fori_loop(0, n_rows, finish_rows, 0)


def spectral_part(tick, n_section, plan, cutoff, lmax, mmax, tokens, cut_table, gains, filters, tables):
    n_rows, n_cols, width = tokens.shape
    fwd, inv, leg, legt = tables
    n_lat, m_local, n_degrees, n_lines = leg.shape
    part = filters.shape[4]
    smem = pl.BlockSpec(memory_space=pltpu.SMEM)
    vmem = pl.BlockSpec(memory_space=pltpu.VMEM)
    anys = pl.BlockSpec(memory_space=pltpu.HBM)
    dma = pltpu.SemaphoreType.DMA
    lonwise = pltpu.VMEM((4, n_rows, LON_PAD, part), BF16)
    latwise = pltpu.VMEM((n_lat, n_rows, MODE_PAD, part), BF16)
    n_groups = len(GROUPS)
    return pl.pallas_call(
        functools.partial(spec_kernel, tick, n_section),
        out_shape=(
            jax.ShapeDtypeStruct((n_rows, n_cols, width), F32),
            jax.ShapeDtypeStruct((n_rows, LON_PAD, width), BF16),
            jax.ShapeDtypeStruct((n_rows, LON_PAD, width), BF16),
        ),
        in_specs=[smem] * 4 + [vmem] * 6 + [anys] * 2,
        out_specs=(anys, anys, anys),
        scratch_shapes=[
            lonwise, lonwise, latwise, latwise,
            pltpu.VMEM((2, n_lines * MODE_PAD, part // 2), F32),
            pltpu.VMEM((2, n_lat * 8 * MODE_PAD, part // 2), F32),
            latwise, latwise, lonwise, lonwise,
            pltpu.VMEM((n_rows, n_cols, width), F32),
            pltpu.VMEM((n_rows, LON_PAD, width), BF16),
            pltpu.VMEM(leg.shape[1:], BF16),
            pltpu.VMEM(legt.shape[1:], BF16),
            dma((4, n_rows)), dma((4, n_rows)),
            dma((n_groups, n_lat)), dma((n_groups, n_lat)),
            dma((n_groups, n_lat)), dma((n_groups, n_lat)),
            dma((4, n_rows)), dma((4, n_rows)),
            dma((n_rows,)), dma((n_rows,)),
            dma((2 + 2 * n_rows,)),
        ],
        compiler_params=pltpu.CompilerParams(
            collective_id=2 * tick, has_side_effects=True, vmem_limit_bytes=VMEM),
        cost_estimate=pl.CostEstimate(flops=5 * 10**10, bytes_accessed=10**7, transcendentals=0),
    )(plan, cutoff, lmax, mmax, tokens, cut_table, gains, filters, fwd, inv, leg, legt)


CHUNKS = 4


def mlp_kernel(
    v_hbm, own_hbm, sib_hbm, w_hbm, out_hbm,
    x_all, wi, wo, acc, given, taken, vbuf, obuf, x_sem, w_sem, v_sem, o_sem, p_send, p_recv,
):
    lon = lax.axis_index("lon")
    sibling = lon_peer(lon, 1)
    n_rows, n_cols, width = v_hbm.shape
    ff = wi.shape[3]
    shard = w_hbm.shape[1] // 2

    barrier = pltpu.get_barrier_semaphore()
    pl.semaphore_signal(barrier, inc=1, device_id={"lon": sibling}, device_id_type=MESH)

    get_x = [
        pltpu.make_async_copy(ref.at[pl.ds(first, count)], x_all.at[pl.ds(n_rows * k + first, count)], x_sem.at[2 * k + g])
        for k, ref in enumerate((sib_hbm, own_hbm))
        for g, (first, count) in enumerate(GROUPS)
    ]

    def get_wi(c):
        return pltpu.make_async_copy(w_hbm.at[:, pl.ds(0, shard), pl.ds(c * ff, ff)], wi.at[c], w_sem.at[0, c])

    def get_wo(c):
        return pltpu.make_async_copy(w_hbm.at[:, pl.ds(shard, shard), pl.ds(c * ff, ff)], wo.at[c], w_sem.at[1, c])

    get_v = pltpu.make_async_copy(v_hbm, vbuf, v_sem)
    get_x[0].start()
    for c in range(CHUNKS):
        get_wi(c).start()
        get_wo(c).start()
        if c == 0:
            get_x[1].start()
    get_x[2].start()
    get_x[3].start()
    get_v.start()
    pl.semaphore_wait(barrier, 1)

    def send(g):
        first, count = GROUPS[g]
        return pltpu.make_async_remote_copy(
            src_ref=given.at[pl.ds(first, count)], dst_ref=taken.at[pl.ds(first, count)],
            send_sem=p_send.at[g], recv_sem=p_recv.at[g], device_id={"lon": sibling}, device_id_type=MESH)

    def put(j):
        return pltpu.make_async_copy(obuf.at[j], out_hbm.at[j], o_sem.at[j])

    for tile in range(4):
        k, g = tile // 2, tile % 2
        first, count = GROUPS[g]
        size = count * LON_PAD
        get_x[tile].wait()

        def body(c, carry, tile=tile, at=n_rows * k + first, count=count, size=size):
            if tile == 0:
                get_wi(c).wait()
                get_wo(c).wait()
            x = x_all[pl.ds(at, count)].reshape(size, width)
            h = jax.nn.gelu(jnp.dot(x, wi[c].reshape(width, ff), preferred_element_type=F32)).astype(BF16)
            out = lax.dot_general(h, wo[c].reshape(width, ff), (((1,), (1,)), ((), ())), preferred_element_type=F32)
            old = jnp.where(c == 0, 0.0, acc[0:size, :])
            acc[0:size, :] = old + out
            return carry

        lax.fori_loop(0, CHUNKS, body, 0)
        total = acc[0:size, :].reshape(count, LON_PAD, width)
        if k == 0:
            given[pl.ds(first, count)] = total.astype(BF16)
            send(g).start()
        else:
            if g == 0:
                get_v.wait()
            send(g).wait_recv()
            for i in range(count):
                j = first + i
                other = taken[j, 0:n_cols, :].astype(F32)
                obuf[j] = (vbuf[j] + (total[i, 0:n_cols, :] + other)).astype(BF16)
                put(j).start()
    for j in range(n_rows):
        put(j).wait()
    for g in range(2):
        send(g).wait_send()


def mlp_part(tick, v, own, sib, weights):
    n_rows, n_cols, width = v.shape
    n_lat, shard, ff = weights.shape
    shard, ff = shard // 2, ff // CHUNKS
    anys = pl.BlockSpec(memory_space=pltpu.HBM)
    dma = pltpu.SemaphoreType.DMA
    most = max(count for _, count in GROUPS)
    return pl.pallas_call(
        mlp_kernel,
        out_shape=jax.ShapeDtypeStruct((n_rows, n_cols, width), BF16),
        in_specs=[anys] * 4,
        out_specs=anys,
        scratch_shapes=[
            pltpu.VMEM((2 * n_rows, LON_PAD, width), BF16),
            pltpu.VMEM((CHUNKS, n_lat, shard, ff), BF16),
            pltpu.VMEM((CHUNKS, n_lat, shard, ff), BF16),
            pltpu.VMEM((most * LON_PAD, width), F32),
            pltpu.VMEM((n_rows, LON_PAD, width), BF16),
            pltpu.VMEM((n_rows, LON_PAD, width), BF16),
            pltpu.VMEM((n_rows, n_cols, width), F32),
            pltpu.VMEM((n_rows, n_cols, width), BF16),
            dma((4,)), dma((2, CHUNKS)), dma(()), dma((n_rows,)), dma((2,)), dma((2,)),
        ],
        compiler_params=pltpu.CompilerParams(
            collective_id=2 * tick + 1, has_side_effects=True, vmem_limit_bytes=VMEM),
        cost_estimate=pl.CostEstimate(flops=10**10, bytes_accessed=10**7, transcendentals=0),
    )(v, own, sib, weights)


def local(state, fresh, cutoff, plan, lmax, mmax, cutoff_table, norm_gains, filters, w_in, w_out):
    section_idx = lax.axis_index("section")
    n_section = lax.axis_size("section")
    n_lat = lax.axis_size("lat")
    n_lon = lax.axis_size("lon")
    n_rows, n_cols, width = fresh.shape
    n_degrees = filters.shape[3]
    tables = [jnp.asarray(t) for t in spectral_tables(n_lat, n_lon, n_rows, n_cols, n_degrees)]
    core = lax.rem(lax.axis_index("lon"), 2)
    ff_half = w_in.shape[3] // 2

    def gathered(tick):
        block = lax.dynamic_index_in_dim(plan[tick], section_idx, 0, keepdims=False)
        zero = jnp.int32(0)
        mine = [
            lax.dynamic_slice(weight, (zero, block, zero, core * ff_half), (1, 1, weight.shape[2], ff_half))[0, 0]
            for weight in (w_in, w_out)
        ]
        return lax.all_gather(jnp.concatenate(mine, 0), "lat", axis=0)

    weights = [gathered(tick) for tick in (0, 1)]

    def run_block(tokens, tick):
        v, own, sib = spectral_part(
            tick, n_section, plan, cutoff, lmax, mmax, tokens, cutoff_table, norm_gains, filters, tables)
        return mlp_part(tick, v, own, sib, weights[tick])

    first_out = run_block(state[0], 0)
    handed = passed_along(first_out, "section", 1)
    entering = jnp.where(section_idx == 0, fresh, handed)
    second_out = run_block(entering, 1)
    return (first_out[None], second_out[None])


def solution(mesh):
    return jax.shard_map(
        local,
        mesh=mesh,
        in_specs=(
            P("section", "lat", "lon", None),
            P("lat", "lon", None),
            P(),
            P(),
            P(),
            P(),
            P(),
            P("section", None, None, None),
            P("section", None, None, None, "lon"),
            P("section", None, "lat", None),
            P("section", None, "lat", None),
        ),
        out_specs=(P("section", "lat", "lon", None), P("section", "lat", "lon", None)),
        check_vma=False,
    )
```

profile of v0, /device:TPU:3, one launch (start us, length us, event | category | flops | bytes accessed | tf_op | source)
XLA Modules:
  0.0 253.4 jit_solution(19208937770279527)
XLA Ops:
  7.2 0.0 copy-start.3
  7.2 0.0 all-gather.5.cloned.1.call-start
  7.2 0.8 fusion
  8.0 0.6 constant_dynamic-slice_fusion
  12.5 1.1 dynamic-slice_bitcast_fusion.1
  13.6 0.0 copy-done.3
  13.6 0.8 pad_maximum_fusion
  14.5 0.0 all-gather.5.cloned.1.call-update
  14.5 0.0 all-gather.7.cloned.1.call-start
  14.5 0.8 pad_maximum_fusion.1
  15.4 0.0 all-gather.7.cloned.1.call-update
  15.4 74.3 %shard_map.158 = (f32[7,90,1024]{2,1,0:T(8,128)}, bf16[7,96,1024]{2,1,0:T(8,128)(2,1)}, bf16[7,96,1024]{2,1,0:T(8,128)(2,1)}) custom-call(s32[2,2]{1,0:T(2,128)} %plan.3, s32[3]{0:T(128)} %cutoff.3, s32[2]{0:T(128)} %lmax.3, s32[2]{0:T(128)} %mmax.3, bf16[7,90,1024]{2,1,0:T(8,128)(2,1)} %bitcast.19, f32[16,1024]{1,0:T(8,128)} %cut_table.3, ...), custom_call_target="tpu_custom_call" | custom-call | flops 49999998976 | bytes 10000000 | tf_op jit(solution)/shard_map/pallas_call | solution.py:313
  89.7 12.2 %all-gather.5.cloned.1.call-done = bf16[2048,2048]{1,0:T(8,128)(2,1)} async-done(((bf16[128,2048]{1,0:T(8,128)(2,1)}), bf16[2048,2048]{1,0:T(8,128)(2,1)}) %all-gather.5.cloned.1.call-update) | async-done | bytes 8388624 | tf_op jit(solution)/shard_map/all_gather | solution.py:477
  101.9 0.0 copy-start
  101.9 20.1 %shard_map.159 = bf16[7,90,1024]{2,1,0:T(8,128)(2,1)} custom-call(f32[7,90,1024]{2,1,0:T(8,128)} %get-tuple-element.8.v_hbm, bf16[7,96,1024]{2,1,0:T(8,128)(2,1)} %get-tuple-element.9.own_hbm, bf16[7,96,1024]{2,1,0:T(8,128)(2,1)} %get-tuple-element.10.sib_hbm, bf16[16,128,2048]{2,1,0:T(8,128)(2,1)} %bitcast.18), custom_call_target="tpu_custom_call" | custom-call | flops 10000000000 | bytes 10000000 | tf_op jit(solution)/shard_map/pallas_call | solution.py:437
  122.0 1.5 collective-permute-start
  123.5 32.0 %collective-permute-done = bf16[7,90,1024]{2,1,0:T(8,128)(2,1)S(1)} collective-permute-done((bf16[7,90,1024]{2,1,0:T(8,128)(2,1)}, bf16[7,90,1024]{2,1,0:T(8,128)(2,1)S(1)}, u32[]{:S(2)}, u32[]{:S(2)}) %collective-permute-start) | collective-permute-done | bytes 1290272 | tf_op jit(solution)/shard_map/ppermute | solution.py:25
  155.5 0.0 copy-done
  155.5 1.2 broadcast_select_fusion.tok
  156.7 66.7 %shard_map.160 = (f32[7,90,1024]{2,1,0:T(8,128)}, bf16[7,96,1024]{2,1,0:T(8,128)(2,1)}, bf16[7,96,1024]{2,1,0:T(8,128)(2,1)}) custom-call(s32[2,2]{1,0:T(2,128)} %plan.3, s32[3]{0:T(128)} %cutoff.3, s32[2]{0:T(128)} %lmax.3, s32[2]{0:T(128)} %mmax.3, bf16[7,90,1024]{2,1,0:T(8,128)(2,1)} %broadcast_select_fusion.tok, f32[16,1024]{1,0:T(8,128)} %cut_table.3, ...), custom_call_target="tpu_custom_call" | custom-call | flops 49999998976 | bytes 10000000 | tf_op jit(solution)/shard_map/pallas_call | solution.py:313
  223.4 0.0 all-gather.7.cloned.1.call-done
  223.4 0.0 copy-start.1
  223.4 20.2 %shard_map.161 = bf16[7,90,1024]{2,1,0:T(8,128)(2,1)} custom-call(f32[7,90,1024]{2,1,0:T(8,128)} %get-tuple-element.11.v_hbm, bf16[7,96,1024]{2,1,0:T(8,128)(2,1)} %get-tuple-element.12.own_hbm, bf16[7,96,1024]{2,1,0:T(8,128)(2,1)} %get-tuple-element.13.sib_hbm, bf16[16,128,2048]{2,1,0:T(8,128)(2,1)} %bitcast.17), custom_call_target="tpu_custom_call" | custom-call | flops 10000000000 | bytes 10000000 | tf_op jit(solution)/shard_map/pallas_call | solution.py:437
  243.6 0.0 copy-done.1
  243.6 0.0 copy-start.2
  243.6 1.1 copy.19
  244.7 0.7 copy-done.2
  245.5 1.1 copy.20
  (1 shorter events, 0.0 us)
Async XLA Ops:
  7.2 6.4 %copy-start.3 = (bf16[1,2,64,4096]{3,2,1,0:T(8,128)(2,1)S(1)}, bf16[1,2,64,4096]{3,2,1,0:T(8,128)(2,1)}, u32[]{:S(2)}) copy-start(bf16[1,2,64,4096]{3,2,1,0:T(8,128)(2,1)} %param.25) | copy-start | bytes 3145732
  7.2 94.7 %all-gather.5.cloned.1.call-start = ((), (), s32[]{:S(2)}) async-start(), calls=%async_computation | async-start | bytes 8912896 | tf_op jit(solution)/shard_map/all_gather | solution.py:477
  14.5 208.9 %all-gather.7.cloned.1.call-start = ((), (), s32[]{:S(2)}) async-start(), calls=%async_computation.1 | async-start | bytes 8912896 | tf_op jit(solution)/shard_map/all_gather | solution.py:477
  101.9 53.6 %copy-start = (bf16[7,90,1024]{2,1,0:T(8,128)(2,1)S(1)}, bf16[7,90,1024]{2,1,0:T(8,128)(2,1)}, u32[]{:S(2)}) copy-start(bf16[7,90,1024]{2,1,0:T(8,128)(2,1)} %param.16) | copy-start | bytes 3870724
  122.0 33.5 %collective-permute-start = (bf16[7,90,1024]{2,1,0:T(8,128)(2,1)}, bf16[7,90,1024]{2,1,0:T(8,128)(2,1)S(1)}, u32[]{:S(2)}, u32[]{:S(2)}) collective-permute-start(bf16[7,90,1024]{2,1,0:T(8,128)(2,1)} %shard_map.159), channel_id=1, source_target_pairs={{0,64},{1,65},{2,66},{3,67},{4,68},{5,69},{6,70},{7,71},{8,72},{9,... | collective-permute-start | bytes 3870728 | tf_op jit(solution)/shard_map/ppermute | solution.py:25
  223.4 20.2 %copy-start.1 = (bf16[7,90,1024]{2,1,0:T(8,128)(2,1)S(1)}, bf16[7,90,1024]{2,1,0:T(8,128)(2,1)}, u32[]{:S(2)}) copy-start(bf16[7,90,1024]{2,1,0:T(8,128)(2,1)} %shard_map.159) | copy-start | bytes 3870724
  243.6 1.8 copy-start.2
Sparse Core Ops, SparseCore 0:
  14.6 87.2 all-gather.4
  104.6 69.9 all-gather.6
where the time goes:
time: 254 us; the launch traced here: 253 us
  Pallas kernels  181 us (71%)
  waiting for transfers between devices  44.3 us (17%)
  between operations  18 us (7%)
  local copies, waits for them, and re-layouts  5.4 us (2%)
  other arithmetic  2.89 us (1%)
    pallas_call x2, Pallas kernels, spectral_part(): pl.pallas_call(functools.partial(spec_kernel, tick, n_section), out_shape...  141 us
    pallas_call x2, Pallas kernels, mlp_part(): pl.pallas_call(mlp_kernel, out_shape=jax.ShapeDtypeStruct((n_rows, n_cols...  40.2 us
    ppermute x1, waiting for transfers between devices, passed_along(): lax.ppermute(value, axis, [(source, source + steps) for source in range(l...  32 us
    all_gather x2, waiting for transfers between devices, gathered(): return lax.all_gather(jnp.concatenate(mine, 0), 'lat', axis=0)  12.2 us
  transfers between devices with their start and end apart: 3, of which 2 were waited for; matrix products, arithmetic and copies ran while one was open for 1% of the time, Pallas kernels for 64%

commit v1 on v0

v1 whole, which is shorter than its diff:
```python
import functools
import math

import jax
import jax.numpy as jnp
import numpy as np
from jax import lax
from jax.experimental import pallas as pl
from jax.experimental.pallas import tpu as pltpu
from jax.sharding import PartitionSpec as P

MM = 96
MESH = pl.DeviceIdType.MESH
BF16 = jnp.bfloat16
F32 = jnp.float32
VMEM = 60 * 1024 * 1024
LON_PAD = 96
MODE_PAD = 16
GROUPS = ((0, 4), (4, 3))
ROWS = ((0, 2), (2, 2), (4, 3))


def passed_along(value, axis, steps):
    count = lax.axis_size(axis)
    leading, last = (max(0, -steps), min(count, count - steps))
    return lax.ppermute(value, axis, [(source, source + steps) for source in range(leading, last)])


def legendre_table(n_orders, n_rows, n_degrees):
    theta = math.pi * (np.arange(n_rows) + 0.5) / n_rows
    cosine, sine = np.cos(theta), np.sin(theta)
    table = np.zeros((n_degrees, n_orders, n_rows))
    for m in range(n_orders):
        log_start = (
            0.5 * math.log((2.0 * m + 1.0) / (4.0 * math.pi))
            + math.lgamma(m + 0.5) - math.lgamma(0.5) - math.lgamma(m + 1.0)
        )
        table[m, m] = np.exp(log_start + m * np.log(sine))
        for l in range(m + 1, n_degrees):
            coef_a = math.sqrt((4.0 * l * l - 1.0) / (l * l - m * m))
            coef_b = math.sqrt(max((l - 1.0) ** 2 - m * m, 0.0) / max(4.0 * (l - 1.0) ** 2 - 1.0, 1.0))
            before = table[l - 2, m] if l - 2 >= m else 0.0
            table[l, m] = coef_a * (cosine * table[l - 1, m] - coef_b * before)
    quad = 2.0 * math.pi * (math.pi / n_rows) * sine
    return table, table * quad


def spectral_tables(n_lat, n_lon, n_rows, n_cols, n_degrees):
    m_local = MM // n_lat
    all_cols = n_cols * n_lon
    phase = 2.0 * math.pi * ((np.arange(all_cols)[:, None] * np.arange(MM)[None, :]) % all_cols) / all_cols
    weight = np.where(np.arange(MM) == 0, 1.0, 2.0)
    forward = np.zeros((n_lat, MODE_PAD, n_lon, LON_PAD))
    inverse = np.zeros((n_lon, LON_PAD, n_lat, MODE_PAD))
    parts = ((np.cos(phase) / all_cols, weight * np.cos(phase)), (-np.sin(phase) / all_cols, -weight * np.sin(phase)))
    for r, (fwd, inv) in enumerate(parts):
        fwd = fwd.reshape(n_lon, n_cols, n_lat, m_local)
        inv = inv.reshape(n_lon, n_cols, n_lat, m_local)
        forward[:, r * m_local : (r + 1) * m_local, :, :n_cols] = fwd.transpose(2, 3, 0, 1)
        inverse[:, :n_cols, :, r * m_local : (r + 1) * m_local] = inv
    forward = forward.reshape(n_lat * MODE_PAD, n_lon * LON_PAD)
    inverse = inverse.reshape(n_lon * LON_PAD, n_lat * MODE_PAD)
    plain, weighted = legendre_table(MM, n_rows * n_lat, n_degrees)
    split = (n_degrees, n_lat, m_local, n_lat, n_rows)
    weighted = weighted.reshape(split).transpose(1, 2, 0, 3, 4).reshape(n_lat, m_local, n_degrees, n_lat * n_rows)
    padded = np.zeros((n_lat, m_local, n_lat, 8, n_degrees))
    padded[:, :, :, :n_rows] = plain.reshape(split).transpose(1, 2, 3, 4, 0)
    padded = padded.reshape(n_lat, m_local, n_lat * 8, n_degrees)
    return tuple(t.astype(BF16) for t in (forward, inverse, weighted, padded))


def layer_norm(values, gain):
    scale = 1.0 / values.shape[-1]
    center = values - jnp.sum(values, axis=-1, keepdims=True) * scale
    spread = jnp.sum(center * center, axis=-1, keepdims=True) * scale
    return center * lax.rsqrt(spread + 1e-05) * gain


def lon_peer(me, d):
    return lax.rem(me // 2 + d // 2, 2) * 2 + lax.rem(lax.rem(me, 2) + d % 2, 2)


def spec_kernel(
    tick, n_section, plan, cutoff, lmax, mmax, *refs,
):
    if tick == 0:
        tok_hbm, prior_hbm, *refs = refs
    else:
        tok_hbm, prior_hbm, other_gains, x_next, *refs = refs
    cut_table, gains, filters, fwd, inv, leg_hbm, legt_hbm, v_out, own_out, sib_out, *refs = refs
    if tick == 0:
        x_next, *refs = refs
    (
        tok, prior, norm, ahead, x_all, spec, y_all, y_f32, f_f32, back, z_all, o_all, r_all, vbuf, nbuf, leg, legt,
        a_send, a_recv, e_send, f_recv, t_send, t_recv, b_send, b_recv, c_send, c_recv, d_send, d_recv, n_send, n_recv, loc, row_in, next_sem,
    ) = refs
    section, lat, lon = (lax.axis_index(a) for a in ("section", "lat", "lon"))
    n_lat = spec.shape[1]
    n_rows, n_cols, width = tok.shape
    n_degrees, part = filters.shape[3], filters.shape[4]
    m_local = leg.shape[0]
    half = part // 2
    sibling = lon_peer(lon, 1)
    handing = tick > 0
    first_section = section == 0

    barrier = pltpu.get_barrier_semaphore()
    greeted = 3 + n_lat - 1
    for d in (1, 2, 3):
        pl.semaphore_signal(barrier, inc=1, device_id={"lon": lon_peer(lon, d)}, device_id_type=MESH)
    if handing:
        greeted += 4
        for q in range(4):
            pl.semaphore_signal(barrier, inc=1, device_id={"section": 1 - section, "lon": q}, device_id_type=MESH)

    def greet(d, carry):
        pl.semaphore_signal(barrier, inc=1, device_id={"lat": lax.rem(lat + d, n_lat)}, device_id_type=MESH)
        return carry

    lax.fori_loop(1, n_lat, greet, 0)

    def get_tok(j):
        return pltpu.make_async_copy(tok_hbm.at[j], tok.at[j], row_in.at[0, j])

    def get_prior(j):
        return pltpu.make_async_copy(prior_hbm.at[j], prior.at[j], row_in.at[1, j])

    def get_next(h):
        return pltpu.make_async_copy(x_next.at[h], x_all.at[h], next_sem.at[h])

    def put_next(h):
        return pltpu.make_async_copy(ahead.at[h, lon], x_next.at[h, lon], next_sem.at[h])

    def over_rows(step):
        def body(j, carry):
            step(j)
            return carry

        lax.fori_loop(0, n_rows, body, 0)

    if handing:

        @pl.when(first_section)
        def _():
            over_rows(lambda j: get_prior(j).start())
            for h in (0, 1):
                get_next(h).start()
            over_rows(lambda j: get_tok(j).start())
    else:
        over_rows(lambda j: get_tok(j).start())

        @pl.when(first_section)
        def _():
            over_rows(lambda j: get_prior(j).start())
    get_leg = pltpu.make_async_copy(leg_hbm.at[lat], leg, loc.at[0])
    get_legt = pltpu.make_async_copy(legt_hbm.at[lat], legt, loc.at[1])
    get_leg.start()
    get_legt.start()

    block = plan[tick, section]
    cut = cutoff[tick - section + n_section - 1]
    l_max, m_max = lmax[section], mmax[section]
    embed = cut_table[pl.ds(cut, 1), :]
    gain_one = gains[0, block, 0:1, :]
    gain_two = gains[0, block, 1:2, :]
    pad = jnp.zeros((2, 4, n_rows, 16, half), BF16)
    ahead[:, :, :, LON_PAD - 16 :, :] = pad
    if not handing:
        norm[:, :, :, LON_PAD - 16 :, :] = pad
    f_f32[...] = jnp.zeros_like(f_f32)
    nbuf[:, LON_PAD - 16 :, :] = jnp.zeros((n_rows, 16, width), BF16)
    pl.semaphore_wait(barrier, greeted)

    def copy_a(h, j, d, sending):
        peer = lon_peer(lon, d)
        slot = lon if sending else peer
        return pltpu.make_async_remote_copy(
            src_ref=norm.at[h, peer, j] if sending else x_all.at[h, slot, j], dst_ref=x_all.at[h, slot, j], send_sem=a_send.at[h, d, j],
            recv_sem=a_recv.at[h, d, j], device_id={"lon": peer}, device_id_type=MESH)

    def copy_e(h, j, d):
        peer = lon_peer(lon, d)
        return pltpu.make_async_remote_copy(
            src_ref=ahead.at[h, peer, j], dst_ref=x_all.at[h, lon, j], send_sem=e_send.at[h, d, j],
            recv_sem=a_recv.at[h, d, j], device_id={"section": 1 - section, "lon": peer}, device_id_type=MESH)

    def copy_f(h, j, d, sending):
        peer = lon_peer(lon, d)
        slot = lon if sending else peer
        return pltpu.make_async_remote_copy(
            src_ref=ahead.at[h, peer, j], dst_ref=x_next.at[h, slot, j], send_sem=e_send.at[h, d, j],
            recv_sem=f_recv.at[h, d, j], device_id={"lon": peer}, device_id_type=MESH)

    def copy_t(j):
        return pltpu.make_async_remote_copy(
            src_ref=prior.at[j], dst_ref=tok.at[j], send_sem=t_send.at[j], recv_sem=t_recv.at[j],
            device_id={"section": 1 - section}, device_id_type=MESH)

    def split_into(dst, j, out):
        for q in range(4):
            for h in (0, 1):
                at = q * part + h * half
                dst[h, q, j, 0:n_cols, :] = out[:, at : at + half]

    def first_norm(j):
        get_tok(j).wait()
        split_into(norm, j, layer_norm(tok[j].astype(F32) + embed, gain_one).astype(BF16))
        for d in (2, 3, 1):
            copy_a(0, j, d, True).start()
        for h in (0, 1):
            x_all[h, lon, j] = norm[h, lon, j]

    def first_norm_rest(j):
        for d in (2, 3, 1):
            copy_a(1, j, d, True).start()

    if handing:

        @pl.when(first_section)
        def _():
            next_block = plan[tick, 1]
            next_embed = cut_table[pl.ds(cutoff[tick - 1 + n_section - 1], 1), :]
            next_gain = other_gains[0, next_block, 0:1, :]

            def norm_ahead(j):
                get_prior(j).wait()
                split_into(ahead, j, layer_norm(prior[j].astype(F32) + next_embed, next_gain).astype(BF16))
                for d in range(4):
                    copy_e(0, j, d).start()

            def norm_ahead_rest(j):
                for d in range(4):
                    copy_e(1, j, d).start()

            over_rows(norm_ahead)
            over_rows(norm_ahead_rest)
            over_rows(lambda j: copy_t(j).start())
    else:
        over_rows(first_norm)
        over_rows(first_norm_rest)

        @pl.when(first_section)
        def _():
            next_block = plan[tick + 1, 0]
            next_embed = cut_table[pl.ds(cutoff[tick + 1 + n_section - 1], 1), :]
            next_gain = gains[0, next_block, 0:1, :]

            def norm_next(j):
                get_prior(j).wait()
                split_into(ahead, j, layer_norm(prior[j].astype(F32) + next_embed, next_gain).astype(BF16))
                for h in (0, 1):
                    for d in (2, 3, 1):
                        copy_f(h, j, d, True).start()

            over_rows(norm_next)
            for h in (0, 1):
                put_next(h).start()

    def moved(src, dst, send, recv, sending, h, d):
        peer = lax.rem(lat + d, n_lat)
        origin = lax.rem(lat - d + n_lat, n_lat)
        where = lat if sending else origin
        return pltpu.make_async_remote_copy(
            src_ref=src.at[h, peer], dst_ref=dst.at[h, where],
            send_sem=send.at[h, d], recv_sem=recv.at[h, d], device_id={"lat": peer}, device_id_type=MESH)

    def over_lat(step):
        def body(d, carry):
            step(d)
            return carry

        lax.fori_loop(1, n_lat, body, 0)

    def take_a(h, j):
        for d in (1, 2, 3):
            copy_a(h, j, d, False).wait_recv()

    def zonal(h, first, count):
        if handing:

            @pl.when(jnp.logical_not(first_section))
            def _():
                for j in range(first, first + count):
                    copy_e(h, j, 0).wait_recv()
                    take_a(h, j)
        else:
            for j in range(first, first + count):
                take_a(h, j)

        wide = jnp.concatenate(
            [x_all[h, :, j].reshape(4 * LON_PAD, half) for j in range(first, first + count)], axis=1)
        out = jnp.dot(fwd[...], wide, preferred_element_type=F32).astype(BF16)
        for i in range(count):
            spec[h, :, first + i] = out[:, i * half : (i + 1) * half].reshape(n_lat, MODE_PAD, half)

    for h in (0, 1):
        if handing:

            @pl.when(first_section)
            def _(h=h):
                get_next(h).wait()

        for first, count in ROWS:
            zonal(h, first, count)
        over_lat(lambda d, h=h: moved(spec, y_all, b_send, b_recv, True, h, d).start())

    rows = n_rows * MODE_PAD
    n_lines = n_lat * n_rows
    degree = lax.broadcasted_iota(jnp.int32, (n_degrees, half), 0)
    get_leg.wait()
    get_legt.wait()

    for h in (0, 1):

        def widen(src, value, h=h):
            at = pl.multiple_of(src * rows, 16)
            y_f32[h, pl.ds(at, rows), :] = value.reshape(rows, half).astype(F32)

        widen(lat, spec[h, lat])

        def take_b(d, h=h):
            moved(spec, y_all, b_send, b_recv, False, h, d).wait_recv()
            origin = lax.rem(lat - d + n_lat, n_lat)
            widen(origin, y_all[h, origin])

        over_lat(take_b)
        fil_re = filters[0, block, 0, :, h * half : (h + 1) * half]
        fil_im = filters[0, block, 1, :, h * half : (h + 1) * half]
        for m in range(m_local):
            pieces = [y_f32[h, pl.ds(r * m_local + m, n_lines, stride=MODE_PAD), :] for r in (0, 1)]
            column = jnp.concatenate(pieces, axis=1).astype(BF16)
            coeff = jnp.dot(leg[m], column, preferred_element_type=F32)
            co_re, co_im = coeff[:, :half], coeff[:, half:]
            order = lat * m_local + m
            keep = (degree < l_max) & (jnp.full((n_degrees, half), order, jnp.int32) < m_max)
            out_re = jnp.where(keep, co_re * fil_re - co_im * fil_im, 0.0)
            out_im = jnp.where(keep, co_re * fil_im + co_im * fil_re, 0.0)
            out = jnp.concatenate([out_re, out_im], axis=1).astype(BF16)
            lines = jnp.dot(legt[m], out, preferred_element_type=F32)
            for r in (0, 1):
                f_f32[h, pl.ds(r * m_local + m, n_lat * 8, stride=MODE_PAD), :] = lines[:, r * half : (r + 1) * half]

        def narrow(peer, h=h):
            at = pl.multiple_of(peer * (8 * MODE_PAD), 16)
            return f_f32[h, pl.ds(at, rows), :].astype(BF16).reshape(n_rows, MODE_PAD, half)

        def send_c(d, h=h):
            peer = lax.rem(lat + d, n_lat)
            back[h, peer] = narrow(peer)
            moved(back, z_all, c_send, c_recv, True, h, d).start()

        over_lat(send_c)
        z_all[h, lat] = narrow(lat)

    def copy_d(h, j, d, sending):
        peer = lon_peer(lon, d)
        slot = lon if sending else peer
        return pltpu.make_async_remote_copy(
            src_ref=o_all.at[h, peer, j], dst_ref=r_all.at[h, slot, j], send_sem=d_send.at[h, d, j],
            recv_sem=d_recv.at[h, d, j], device_id={"lon": peer}, device_id_type=MESH)

    for h in (0, 1):
        over_lat(lambda d, h=h: moved(back, z_all, c_send, c_recv, False, h, d).wait_recv())
        for first, count in ROWS:
            modes = jnp.concatenate(
                [z_all[h, :, j].reshape(n_lat * MODE_PAD, half) for j in range(first, first + count)], axis=1)
            out = jnp.dot(inv[...], modes, preferred_element_type=F32).astype(BF16)
            for i in range(count):
                j = first + i
                o_all[h, :, j] = out[:, i * half : (i + 1) * half].reshape(4, LON_PAD, half)
                for d in (2, 3, 1):
                    copy_d(h, j, d, True).start()
                r_all[h, lon, j] = o_all[h, lon, j]

    def put_v(j):
        return pltpu.make_async_copy(vbuf.at[j], v_out.at[j], loc.at[2 + j])

    def put_own(j):
        return pltpu.make_async_copy(nbuf.at[j], own_out.at[j], loc.at[2 + n_rows + j])

    def put_sib(j):
        return pltpu.make_async_remote_copy(
            src_ref=nbuf.at[j], dst_ref=sib_out.at[j], send_sem=n_send.at[j], recv_sem=n_recv.at[j],
            device_id={"lon": sibling}, device_id_type=MESH)

    if handing:

        @pl.when(jnp.logical_not(first_section))
        def _():
            over_rows(lambda j: copy_t(j).wait_recv())

        @pl.when(first_section)
        def _():
            over_rows(lambda j: get_tok(j).wait())

    def second_norm(j):
        for h in (0, 1):
            for d in (1, 2, 3):
                copy_d(h, j, d, False).wait_recv()
        spectral = jnp.concatenate(
            [r_all[h, q, j, 0:n_cols, :] for q in range(4) for h in (0, 1)], axis=1).astype(F32)
        mixed = tok[j].astype(F32) + embed + spectral
        vbuf[j] = mixed
        nbuf[j, 0:n_cols, :] = layer_norm(mixed, gain_two).astype(BF16)
        put_sib(j).start()
        put_v(j).start()
        put_own(j).start()

    over_rows(second_norm)

    def finish_a(j):
        for h in (0, 1):
            for d in (1, 2, 3):
                copy_a(h, j, d, True).wait_send()

    def finish_rows(j):
        for h in (0, 1):
            for d in (1, 2, 3):
                copy_d(h, j, d, True).wait_send()
        put_v(j).wait()
        put_own(j).wait()
        put_sib(j).wait()

    def finish_lat(d):
        for h in (0, 1):
            moved(spec, y_all, b_send, b_recv, True, h, d).wait_send()
            moved(back, z_all, c_send, c_recv, True, h, d).wait_send()

    if handing:

        def finish_handing(j):
            for h in (0, 1):
                for d in range(4):
                    copy_e(h, j, d).wait_send()
            copy_t(j).wait_send()

        @pl.when(first_section)
        def _():
            over_rows(finish_handing)
    else:

        def finish_next(j):
            for h in (0, 1):
                for d in (1, 2, 3):
                    copy_f(h, j, d, True).wait_send()
                    copy_f(h, j, d, False).wait_recv()

        @pl.when(first_section)
        def _():
            over_rows(finish_next)
            for h in (0, 1):
                put_next(h).wait()

        over_rows(finish_a)
    over_lat(finish_lat)
    over_rows(finish_rows)


def spectral_part(tick, n_section, plan, cutoff, lmax, mmax, tokens, cut_table, gains, filters, tables, prior=()):
    n_rows, n_cols, width = tokens.shape
    fwd, inv, leg, legt = tables
    n_lat, m_local, n_degrees, n_lines = leg.shape
    part = filters.shape[4]
    half = part // 2
    smem = pl.BlockSpec(memory_space=pltpu.SMEM)
    vmem = pl.BlockSpec(memory_space=pltpu.VMEM)
    anys = pl.BlockSpec(memory_space=pltpu.HBM)
    dma = pltpu.SemaphoreType.DMA
    lonwise = pltpu.VMEM((2, 4, n_rows, LON_PAD, half), BF16)
    latwise = pltpu.VMEM((2, n_lat, n_rows, MODE_PAD, half), BF16)
    small = pltpu.VMEM((16, 128), BF16)
    tokens_buf = pltpu.VMEM((n_rows, n_cols, width), BF16)
    return pl.pallas_call(
        functools.partial(spec_kernel, tick, n_section),
        out_shape=(
            jax.ShapeDtypeStruct((n_rows, n_cols, width), F32),
            jax.ShapeDtypeStruct((n_rows, LON_PAD, width), BF16),
            jax.ShapeDtypeStruct((n_rows, LON_PAD, width), BF16),
        ) + (() if tick else (jax.ShapeDtypeStruct(lonwise.shape, BF16),)),
        in_specs=[smem] * 4 + [anys] * 2 + ([vmem, anys] if tick else []) + [vmem] * 5 + [anys] * 2,
        out_specs=(anys,) * (3 if tick else 4),
        scratch_shapes=[
            tokens_buf, tokens_buf, small if tick else lonwise, lonwise, lonwise, latwise, latwise,
            pltpu.VMEM((2, n_lines * MODE_PAD, half), F32),
            pltpu.VMEM((2, n_lat * 8 * MODE_PAD, half), F32),
            latwise, latwise, lonwise, lonwise,
            pltpu.VMEM((n_rows, n_cols, width), F32),
            pltpu.VMEM((n_rows, LON_PAD, width), BF16),
            pltpu.VMEM(leg.shape[1:], BF16),
            pltpu.VMEM(legt.shape[1:], BF16),
            dma((2, 4, n_rows)), dma((2, 4, n_rows)), dma((2, 4, n_rows)), dma((2, 4, n_rows)),
            dma((n_rows,)), dma((n_rows,)),
            dma((2, n_lat)), dma((2, n_lat)),
            dma((2, n_lat)), dma((2, n_lat)),
            dma((2, 4, n_rows)), dma((2, 4, n_rows)),
            dma((n_rows,)), dma((n_rows,)),
            dma((2 + 2 * n_rows,)), dma((2, n_rows)), dma((2,)),
        ],
        compiler_params=pltpu.CompilerParams(
            collective_id=2 * tick, has_side_effects=True, vmem_limit_bytes=VMEM),
        cost_estimate=pl.CostEstimate(flops=5 * 10**10, bytes_accessed=10**7, transcendentals=0),
    )(plan, cutoff, lmax, mmax, tokens, *prior, cut_table, gains, filters, fwd, inv, leg, legt)


CHUNKS = 2
LATER = 2


def mlp_kernel(
    v_hbm, own_hbm, sib_hbm, w_hbm, out_hbm,
    x_all, wi, wo, acc, given, taken, vbuf, obuf, x_sem, w_sem, v_sem, o_sem, p_send, p_recv,
):
    lon = lax.axis_index("lon")
    sibling = lon_peer(lon, 1)
    n_rows, n_cols, width = v_hbm.shape
    ff = wi.shape[2]
    part = ff // CHUNKS
    shard = w_hbm.shape[1] // 2

    barrier = pltpu.get_barrier_semaphore()
    pl.semaphore_signal(barrier, inc=1, device_id={"lon": sibling}, device_id_type=MESH)

    get_x = [
        pltpu.make_async_copy(ref.at[pl.ds(first, count)], x_all.at[pl.ds(n_rows * k + first, count)], x_sem.at[2 * k + g])
        for k, ref in enumerate((sib_hbm, own_hbm))
        for g, (first, count) in enumerate(GROUPS)
    ]

    def get_wi(c):
        return pltpu.make_async_copy(w_hbm.at[:, pl.ds(0, shard), pl.ds(c * part, part)], wi.at[:, :, pl.ds(c * part, part)], w_sem.at[0, c])

    def get_wo(c):
        return pltpu.make_async_copy(w_hbm.at[:, pl.ds(shard, shard), pl.ds(c * part, part)], wo.at[:, :, pl.ds(c * part, part)], w_sem.at[1, c])

    get_v = pltpu.make_async_copy(v_hbm, vbuf, v_sem)
    get_x[0].start()
    for c in range(CHUNKS):
        get_wi(c).start()
        get_wo(c).start()
        if c == 0:
            get_x[1].start()
    get_x[2].start()
    get_x[3].start()
    get_v.start()
    pl.semaphore_wait(barrier, 1)

    def send(g):
        first, count = GROUPS[g]
        return pltpu.make_async_remote_copy(
            src_ref=given.at[pl.ds(first, count)], dst_ref=taken.at[pl.ds(first, count)],
            send_sem=p_send.at[g], recv_sem=p_recv.at[g], device_id={"lon": sibling}, device_id_type=MESH)

    def put(j):
        return pltpu.make_async_copy(obuf.at[j], out_hbm.at[j], o_sem.at[j])

    for tile in range(4):
        k, g = tile // 2, tile % 2
        first, count = GROUPS[g]
        size = count * LON_PAD
        get_x[tile].wait()

        x = x_all[pl.ds(n_rows * k + first, count)].reshape(size, width)
        pieces = CHUNKS if tile == 0 else LATER
        wide = ff // pieces
        for c in range(pieces):
            if tile == 0:
                get_wi(c).wait()
            at = c * wide
            before = jnp.dot(x, wi[:, :, at : at + wide].reshape(width, wide), preferred_element_type=F32)
            h = jax.nn.gelu(before).astype(BF16)
            if tile == 0:
                get_wo(c).wait()
            out = lax.dot_general(
                h, wo[:, :, at : at + wide].reshape(width, wide), (((1,), (1,)), ((), ())), preferred_element_type=F32)
            acc[0:size, :] = out if c == 0 else acc[0:size, :] + out
        total = acc[0:size, :].reshape(count, LON_PAD, width)
        if k == 0:
            given[pl.ds(first, count)] = total.astype(BF16)
            send(g).start()
        else:
            if g == 0:
                get_v.wait()
            send(g).wait_recv()
            for i in range(count):
                j = first + i
                other = taken[j, 0:n_cols, :].astype(F32)
                obuf[j] = (vbuf[j] + (total[i, 0:n_cols, :] + other)).astype(BF16)
                put(j).start()
    for j in range(n_rows):
        put(j).wait()
    for g in range(2):
        send(g).wait_send()


def mlp_part(tick, v, own, sib, weights):
    n_rows, n_cols, width = v.shape
    n_lat, shard, ff = weights.shape
    shard = shard // 2
    anys = pl.BlockSpec(memory_space=pltpu.HBM)
    dma = pltpu.SemaphoreType.DMA
    most = max(count for _, count in GROUPS)
    return pl.pallas_call(
        mlp_kernel,
        out_shape=jax.ShapeDtypeStruct((n_rows, n_cols, width), BF16),
        in_specs=[anys] * 4,
        out_specs=anys,
        scratch_shapes=[
            pltpu.VMEM((2 * n_rows, LON_PAD, width), BF16),
            pltpu.VMEM((n_lat, shard, ff), BF16),
            pltpu.VMEM((n_lat, shard, ff), BF16),
            pltpu.VMEM((most * LON_PAD, width), F32),
            pltpu.VMEM((n_rows, LON_PAD, width), BF16),
            pltpu.VMEM((n_rows, LON_PAD, width), BF16),
            pltpu.VMEM((n_rows, n_cols, width), F32),
            pltpu.VMEM((n_rows, n_cols, width), BF16),
            dma((4,)), dma((2, CHUNKS)), dma(()), dma((n_rows,)), dma((2,)), dma((2,)),
        ],
        compiler_params=pltpu.CompilerParams(
            collective_id=2 * tick + 1, has_side_effects=True, vmem_limit_bytes=VMEM),
        cost_estimate=pl.CostEstimate(flops=10**10, bytes_accessed=10**7, transcendentals=0),
    )(v, own, sib, weights)


def pick_kernel(plan, w_in, w_out, first, second, sem):
    section = lax.axis_index("section")
    core = lax.rem(lax.axis_index("lon"), 2)
    shard, ff = w_in.shape[2], w_in.shape[3] // 2
    columns = pl.ds(pl.multiple_of(core * ff, ff), ff)
    copies = [
        pltpu.make_async_copy(ref.at[0, plan[tick, section], :, columns], out.at[pl.ds(k * shard, shard)], sem.at[tick, k])
        for tick, out in enumerate((first, second))
        for k, ref in enumerate((w_in, w_out))
    ]
    for copy in copies:
        copy.start()
    for copy in copies:
        copy.wait()


def own_weights(plan, w_in, w_out):
    anys = pl.BlockSpec(memory_space=pltpu.HBM)
    out = jax.ShapeDtypeStruct((2 * w_in.shape[2], w_in.shape[3] // 2), BF16)
    return pl.pallas_call(
        pick_kernel,
        out_shape=(out, out),
        in_specs=[pl.BlockSpec(memory_space=pltpu.SMEM), anys, anys],
        out_specs=(pl.BlockSpec(memory_space=pltpu.VMEM),) * 2,
        scratch_shapes=[pltpu.SemaphoreType.DMA((2, 2))],
        compiler_params=pltpu.CompilerParams(vmem_limit_bytes=VMEM),
    )(plan, w_in, w_out)


def local(state, fresh, cutoff, plan, lmax, mmax, cutoff_table, norm_gains, filters, w_in, w_out):
    n_section = lax.axis_size("section")
    n_lat = lax.axis_size("lat")
    n_lon = lax.axis_size("lon")
    n_rows, n_cols, width = fresh.shape
    n_degrees = filters.shape[3]
    tables = [jnp.asarray(t) for t in spectral_tables(n_lat, n_lon, n_rows, n_cols, n_degrees)]
    weights = [lax.all_gather(mine, "lat", axis=0) for mine in own_weights(plan, w_in, w_out)]
    other_gains = passed_along(norm_gains, "section", -1)

    def spectral(tick, tokens, *more):
        return spectral_part(
            tick, n_section, plan, cutoff, lmax, mmax, tokens, cutoff_table, norm_gains, filters, tables, more)

    *parts, entering = spectral(0, state[0], fresh)
    first_out = mlp_part(0, *parts, weights[0])
    parts = spectral(1, fresh, first_out, other_gains, entering)
    second_out = mlp_part(1, *parts, weights[1])
    return (first_out[None], second_out[None])


def solution(mesh):
    return jax.shard_map(
        local,
        mesh=mesh,
        in_specs=(
            P("section", "lat", "lon", None),
            P("lat", "lon", None),
            P(),
            P(),
            P(),
            P(),
            P(),
            P("section", None, None, None),
            P("section", None, None, None, "lon"),
            P("section", None, "lat", None),
            P("section", None, "lat", None),
        ),
        out_specs=(P("section", "lat", "lon", None), P("section", "lat", "lon", None)),
        check_vma=False,
    )
```

time: 254 us -> 219 us (0.86)
  waiting for transfers between devices: 44.3 us -> 24.4 us
  Pallas kernels: 181 us -> 174 us
  between operations: 18 us -> 14.1 us
  other arithmetic: 2.89 us -> 0 us
    ppermute x1, waiting for transfers between devices: 32 us -> 0.01 us  [passed_along(): lax.ppermute(value, axis, [(source, source + steps) for source in range(l...]
    all_gather x2, waiting for transfers between devices: 12.2 us -> 23.7 us  [local(): lax.all_gather(mine, 'lat', axis=0)]
    pallas_call x2, Pallas kernels: 40.2 us -> 34 us  [mlp_part(): pl.pallas_call(mlp_kernel, out_shape=jax.ShapeDtypeStruct((n_rows, n_cols...]
    pallas_call x2, Pallas kernels: 141 us -> 137 us  [spectral_part(): pl.pallas_call(functools.partial(spec_kernel, tick, n_section), out_shape...]
    pallas_call x0 -> x1, Pallas kernels: none -> 2.89 us  [own_weights(): pl.pallas_call(pick_kernel, out_shape=(out, out), in_specs=[pl.BlockSpec(...]
  transfers between devices with their start and end apart: 3 -> 3, of which waited for: 2 -> 2; matrix products, arithmetic and copies ran while one was open for 1% -> 0% of each run, Pallas kernels for 64% -> 71%
where the time goes in v1:
time: 219 us; the launch traced here: 218 us
  Pallas kernels  174 us (79%)
  waiting for transfers between devices  24.4 us (11%)
  between operations  14.1 us (6%)
  local copies, waits for them, and re-layouts  3.52 us (2%)
    pallas_call x2, Pallas kernels, spectral_part(): pl.pallas_call(functools.partial(spec_kernel, tick, n_section), out_shape...  137 us
    pallas_call x2, Pallas kernels, mlp_part(): pl.pallas_call(mlp_kernel, out_shape=jax.ShapeDtypeStruct((n_rows, n_cols...  34 us
    all_gather x2, waiting for transfers between devices, local(): lax.all_gather(mine, 'lat', axis=0)  23.7 us
  transfers between devices with their start and end apart: 3, of which 2 were waited for; matrix products, arithmetic and copies ran while one was open for 0% of the time, Pallas kernels for 71%

profile of v1, /device:TPU:3, one launch (start us, length us, event | category | flops | bytes accessed | tf_op | source)
XLA Modules:
  0.0 217.8 jit_solution(17877304205570488642)
XLA Ops:
  7.2 0.0 copy-start.2
  7.2 0.0 all-gather.5.cloned.1.call-start
  7.2 2.9 %shard_map.159 = (bf16[128,2048]{1,0:T(8,128)(2,1)}, bf16[128,2048]{1,0:T(8,128)(2,1)}) custom-call(s32[2,2]{1,0:T(2,128)} %plan.5, bf16[1,2,64,4096]{3,2,1,0:T(8,128)(2,1)} %w_in.1, bf16[1,2,64,4096]{3,2,1,0:T(8,128)(2,1)} %w_out.1), custom_call_target="tpu_custom_call" | custom-call | tf_op jit(solution)/shard_map/pallas_call | solution.py:643
  10.1 0.0 all-gather.5.cloned.1.call-update
  10.1 0.0 all-gather.7.cloned.1.call-start
  10.2 0.7 all-gather.7.cloned.1.call-update
  10.9 0.0 copy-done.2
  10.9 1.3 collective-permute-start
  12.3 65.0 %shard_map.158 = (f32[7,90,1024]{2,1,0:T(8,128)}, bf16[7,96,1024]{2,1,0:T(8,128)(2,1)}, bf16[7,96,1024]{2,1,0:T(8,128)(2,1)}, bf16[2,4,7,96,128]{4,3,2,1,0:T(8,128)(2,1)}) custom-call(s32[2,2]{1,0:T(2,128)} %plan.5, s32[3]{0:T(128)} %cutoff.3, s32[2]{0:T(128)} %lmax.3, s32[2]{0:T(128)} %mmax.3, bf16[7,90,1024]{2,1,0:T(8,128)(2,1)} %bitcast.9, ...), custom_call_target="tpu_custom_call" | custom-call | flops 49999998976 | bytes 10000000 | tf_op jit(solution)/shard_map/pallas_call | solution.py:473
  77.3 22.0 %all-gather.5.cloned.1.call-done = bf16[2048,2048]{1,0:T(8,128)(2,1)} async-done(((bf16[128,2048]{1,0:T(8,128)(2,1)}), bf16[2048,2048]{1,0:T(8,128)(2,1)}) %all-gather.5.cloned.1.call-update) | async-done | bytes 8388624 | tf_op jit(solution)/shard_map/all_gather | solution.py:660
  99.3 17.1 %shard_map.160.refs_1_ = bf16[7,90,1024]{2,1,0:T(8,128)(2,1)} custom-call(f32[7,90,1024]{2,1,0:T(8,128)} %get-tuple-element.11.v_hbm, bf16[7,96,1024]{2,1,0:T(8,128)(2,1)} %get-tuple-element.12.own_hbm, bf16[7,96,1024]{2,1,0:T(8,128)(2,1)} %get-tuple-element.13.sib_hbm, bf16[16,128,2048]{2,1,0:T(8,128)(2,1)} %bitcast.8), custom_call_target="tpu_custom_call" | custom-call | flops 10000000000 | bytes 10000000 | tf_op jit(solution)/shard_map/pallas_call | solution.py:602
  116.4 0.0 collective-permute-done.refs_2_
  116.4 0.0 copy-start.3
  116.4 0.6 copy-done.3
  117.0 72.3 %shard_map.161 = (f32[7,90,1024]{2,1,0:T(8,128)}, bf16[7,96,1024]{2,1,0:T(8,128)(2,1)}, bf16[7,96,1024]{2,1,0:T(8,128)(2,1)}) custom-call(s32[2,2]{1,0:T(2,128)} %plan.5, s32[3]{0:T(128)} %cutoff.3, s32[2]{0:T(128)} %lmax.3, s32[2]{0:T(128)} %mmax.3, bf16[7,90,1024]{2,1,0:T(8,128)(2,1)} %refs_0_.1, bf16[7,90,1024]{2,1,0:T(8,128)(2,1)} %shard_map.160.refs_1_, ...), custom_call_target="tpu_custom_call" | custom-call | flops 49999998976 | bytes 10000000 | tf_op jit(solution)/shard_map/pallas_call | solution.py:473
  189.3 1.7 all-gather.7.cloned.1.call-done
  191.0 0.0 copy-start
  191.0 16.9 %shard_map.162 = bf16[7,90,1024]{2,1,0:T(8,128)(2,1)} custom-call(f32[7,90,1024]{2,1,0:T(8,128)} %get-tuple-element.16.v_hbm, bf16[7,96,1024]{2,1,0:T(8,128)(2,1)} %get-tuple-element.17.own_hbm, bf16[7,96,1024]{2,1,0:T(8,128)(2,1)} %get-tuple-element.18.sib_hbm, bf16[16,128,2048]{2,1,0:T(8,128)(2,1)} %bitcast.7), custom_call_target="tpu_custom_call" | custom-call | flops 10000000000 | bytes 10000000 | tf_op jit(solution)/shard_map/pallas_call | solution.py:602
  208.0 0.0 copy-done
  208.0 0.0 copy-start.1
  208.0 1.1 copy.19
  209.1 0.7 copy-done.1
  209.8 1.1 copy.20
Async XLA Ops:
  7.2 3.7 %copy-start.2 = (f32[1,2,2,1024]{3,2,1,0:T(2,128)S(1)}, f32[1,2,2,1024]{3,2,1,0:T(2,128)}, u32[]{:S(2)}) copy-start(f32[1,2,2,1024]{3,2,1,0:T(2,128)} %refs_5_.2) | copy-start | bytes 49156
  7.2 92.1 %all-gather.5.cloned.1.call-start = ((), (), s32[]{:S(2)}) async-start(), calls=%async_computation | async-start | bytes 8912896 | tf_op jit(solution)/shard_map/all_gather | solution.py:660
  10.1 180.9 %all-gather.7.cloned.1.call-start = ((), (), s32[]{:S(2)}) async-start(), calls=%async_computation.1 | async-start | bytes 8912896 | tf_op jit(solution)/shard_map/all_gather | solution.py:660
  10.9 105.5 %collective-permute-start = (f32[1,2,2,1024]{3,2,1,0:T(2,128)S(1)}, f32[1,2,2,1024]{3,2,1,0:T(2,128)S(1)}, u32[]{:S(2)}, u32[]{:S(2)}) collective-permute-start(f32[1,2,2,1024]{3,2,1,0:T(2,128)S(1)} %copy-done.2), channel_id=1, source_target_pairs={{64,0},{65,1},{66,2},{67,3},{68,4},{69,5},{70,6},{71,7},{72,8},{73... | collective-permute-start | bytes 49160 | tf_op jit(solution)/shard_map/ppermute | solution.py:26
  116.4 0.6 copy-start.3
  191.0 17.0 %copy-start = (bf16[7,90,1024]{2,1,0:T(8,128)(2,1)S(1)}, bf16[7,90,1024]{2,1,0:T(8,128)(2,1)}, u32[]{:S(2)}) copy-start(bf16[7,90,1024]{2,1,0:T(8,128)(2,1)} %shard_map.160.refs_1_) | copy-start | bytes 3870724
  208.0 1.8 copy-start.1
Sparse Core Ops, SparseCore 0:
  10.7 88.4 all-gather.4
  102.0 89.0 all-gather.6

commit v2 on v1

--- a/solution.py
+++ b/solution.py
@@ -69,11 +69,17 @@
     return tuple(t.astype(BF16) for t in (forward, inverse, weighted, padded))
 
 
+def normed_parts(values):
+    scale = 1.0 / values.shape[-1]
+    mean = jnp.sum(values, axis=-1, keepdims=True) * scale
+    center = values - mean
+    spread = jnp.sum(center * center, axis=-1, keepdims=True) * scale
+    return center, mean, lax.rsqrt(spread + 1e-05)
+
+
 def layer_norm(values, gain):
-    scale = 1.0 / values.shape[-1]
-    center = values - jnp.sum(values, axis=-1, keepdims=True) * scale
-    spread = jnp.sum(center * center, axis=-1, keepdims=True) * scale
-    return center * lax.rsqrt(spread + 1e-05) * gain
+    center, _, scale = normed_parts(values)
+    return center * scale * gain
 
 
 def lon_peer(me, d):
@@ -93,6 +99,7 @@
     (
         tok, prior, norm, ahead, x_all, spec, y_all, y_f32, f_f32, back, z_all, o_all, r_all, vbuf, nbuf, leg, legt,
         a_send, a_recv, e_send, f_recv, t_send, t_recv, b_send, b_recv, c_send, c_recv, d_send, d_recv, n_send, n_recv, loc, row_in, next_sem,
+        stat, stat_all, raw_in, stat_send, stat_recv, raw_send, raw_recv,
     ) = refs
     section, lat, lon = (lax.axis_index(a) for a in ("section", "lat", "lon"))
     n_lat = spec.shape[1]
@@ -191,10 +198,25 @@
             src_ref=ahead.at[h, peer, j], dst_ref=x_next.at[h, slot, j], send_sem=e_send.at[h, d, j],
             recv_sem=f_recv.at[h, d, j], device_id={"lon": peer}, device_id_type=MESH)
 
+    chip = lon // 2
+    far = pl.ds(pl.multiple_of((1 - chip) * 2 * part, part), 2 * part)
+
     def copy_t(j):
         return pltpu.make_async_remote_copy(
-            src_ref=prior.at[j], dst_ref=tok.at[j], send_sem=t_send.at[j], recv_sem=t_recv.at[j],
+            src_ref=prior.at[j, :, far], dst_ref=tok.at[j, :, far], send_sem=t_send.at[j], recv_sem=t_recv.at[j],
             device_id={"section": 1 - section}, device_id_type=MESH)
+
+    def copy_stat(d, sending):
+        peer = lon_peer(lon, d)
+        slot = lon if sending else peer
+        return pltpu.make_async_remote_copy(
+            src_ref=stat, dst_ref=stat_all.at[slot], send_sem=stat_send.at[d], recv_sem=stat_recv.at[d],
+            device_id={"section": 1 - section, "lon": peer}, device_id_type=MESH)
+
+    def copy_raw(h):
+        return pltpu.make_async_remote_copy(
+            src_ref=x_all.at[h, sibling], dst_ref=raw_in.at[h], send_sem=raw_send.at[h], recv_sem=raw_recv.at[h],
+            device_id={"lon": sibling}, device_id_type=MESH)
 
     def split_into(dst, j, out):
         for q in range(4):
@@ -222,17 +244,31 @@
             next_embed = cut_table[pl.ds(cutoff[tick - 1 + n_section - 1], 1), :]
             next_gain = other_gains[0, next_block, 0:1, :]
 
+            stat[...] = jnp.zeros_like(stat)
+            lane = lax.broadcasted_iota(jnp.int32, (n_cols, stat.shape[1]), 1)
+
             def norm_ahead(j):
                 get_prior(j).wait()
-                split_into(ahead, j, layer_norm(prior[j].astype(F32) + next_embed, next_gain).astype(BF16))
+                raw = prior[j].astype(F32)
+                center, mean, scale = normed_parts(raw + next_embed)
+                out = center * scale * next_gain
+                for q in range(4):
+                    at = slice(q * part, (q + 1) * part)
+                    mixed = jnp.where(chip == q // 2, raw[:, at], out[:, at]).astype(BF16)
+                    for h in (0, 1):
+                        ahead[h, q, j, 0:n_cols, :] = mixed[:, h * half : (h + 1) * half]
                 for d in range(4):
                     copy_e(0, j, d).start()
+                old = stat[0:n_cols, :]
+                stat[0:n_cols, :] = jnp.where(lane == 2 * j, mean, jnp.where(lane == 2 * j + 1, scale, old))
 
             def norm_ahead_rest(j):
                 for d in range(4):
                     copy_e(1, j, d).start()
 
             over_rows(norm_ahead)
+            for d in (0, 1):
+                copy_stat(d, True).start()
             over_rows(norm_ahead_rest)
             over_rows(lambda j: copy_t(j).start())
     else:
@@ -274,6 +310,24 @@
     def take_a(h, j):
         for d in (1, 2, 3):
             copy_a(h, j, d, False).wait_recv()
+
+    def of_lon(row, h):
+        out = row[:, h * half : (h + 1) * half]
+        for q in (1, 2, 3):
+            out = jnp.where(lon == q, row[:, q * part + h * half : q * part + (h + 1) * half], out)
+        return out
+
+    def arrived(h, j):
+        if not handing:
+            return x_all[h, :, j].reshape(4 * LON_PAD, half)
+        shift, gain = of_lon(embed, h), of_lon(gain_one, h)
+        rows_of = []
+        for q in range(4):
+            raw = x_all[h, q, j].astype(F32)
+            out = (raw + shift - stat_all[q, :, 2 * j : 2 * j + 1]) * stat_all[q, :, 2 * j + 1 : 2 * j + 2] * gain
+            is_raw = jnp.logical_and(section > 0, chip == q // 2)
+            rows_of.append(jnp.where(is_raw, out, raw).astype(BF16))
+        return jnp.concatenate(rows_of, axis=0)
 
     def zonal(h, first, count):
         if handing:
@@ -287,8 +341,7 @@
             for j in range(first, first + count):
                 take_a(h, j)
 
-        wide = jnp.concatenate(
-            [x_all[h, :, j].reshape(4 * LON_PAD, half) for j in range(first, first + count)], axis=1)
+        wide = jnp.concatenate([arrived(h, j) for j in range(first, first + count)], axis=1)
         out = jnp.dot(fwd[...], wide, preferred_element_type=F32).astype(BF16)
         for i in range(count):
             spec[h, :, first + i] = out[:, i * half : (i + 1) * half].reshape(n_lat, MODE_PAD, half)
@@ -300,8 +353,21 @@
             def _(h=h):
                 get_next(h).wait()
 
+            if h == 0:
+
+                @pl.when(jnp.logical_not(first_section))
+                def _():
+                    for d in (0, 1):
+                        copy_stat(d, False).wait_recv()
+
         for first, count in ROWS:
             zonal(h, first, count)
+        if handing:
+
+            @pl.when(jnp.logical_not(first_section))
+            def _(h=h):
+                copy_raw(h).start()
+
         over_lat(lambda d, h=h: moved(spec, y_all, b_send, b_recv, True, h, d).start())
 
     rows = n_rows * MODE_PAD
@@ -387,7 +453,18 @@
 
         @pl.when(jnp.logical_not(first_section))
         def _():
-            over_rows(lambda j: copy_t(j).wait_recv())
+            for h in (0, 1):
+                copy_raw(h).wait_recv()
+
+            def assemble(j):
+                copy_t(j).wait_recv()
+                for h in (0, 1):
+                    mine = pl.ds(pl.multiple_of(lon * part + h * half, half), half)
+                    other = pl.ds(pl.multiple_of(sibling * part + h * half, half), half)
+                    tok[j, :, mine] = x_all[h, lon, j, 0:n_cols, :]
+                    tok[j, :, other] = raw_in[h, j, 0:n_cols, :]
+
+            over_rows(assemble)
 
         @pl.when(first_section)
         def _():
@@ -437,6 +514,13 @@
         @pl.when(first_section)
         def _():
             over_rows(finish_handing)
+            for d in (0, 1):
+                copy_stat(d, True).wait_send()
+
+        @pl.when(jnp.logical_not(first_section))
+        def _():
+            for h in (0, 1):
+                copy_raw(h).wait_send()
     else:
 
         def finish_next(j):
@@ -495,6 +579,10 @@
             dma((2, 4, n_rows)), dma((2, 4, n_rows)),
             dma((n_rows,)), dma((n_rows,)),
             dma((2 + 2 * n_rows,)), dma((2, n_rows)), dma((2,)),
+            pltpu.VMEM((LON_PAD, 128), F32),
+            pltpu.VMEM((4, LON_PAD, 128), F32),
+            pltpu.VMEM((2, n_rows, LON_PAD, half), BF16) if tick else small,
+            dma((2,)), dma((2,)), dma((2,)), dma((2,)),
         ],
         compiler_params=pltpu.CompilerParams(
             collective_id=2 * tick, has_side_effects=True, vmem_limit_bytes=VMEM),

time: 219 us -> 227 us (1.037); the launches traced: 218 us -> 222 us
  Pallas kernels: 174 us -> 180 us
    pallas_call x2, Pallas kernels: 137 us -> 143 us  [spectral_part(): pl.pallas_call(functools.partial(spec_kernel, tick, n_section), out_shape...]
  transfers between devices with their start and end apart: 3 -> 3, of which waited for: 2 -> 1; matrix products, arithmetic and copies ran while one was open for 0% -> 0% of each run, Pallas kernels for 71% -> 72%
where the time goes in v2:
time: 227 us; the launch traced here: 222 us
  Pallas kernels  180 us (79%)
  waiting for transfers between devices  22.5 us (10%)
  between operations  14.5 us (6%)
  local copies, waits for them, and re-layouts  3.52 us (2%)
    pallas_call x2, Pallas kernels, spectral_part(): pl.pallas_call(functools.partial(spec_kernel, tick, n_section), out_shape...  143 us
    pallas_call x2, Pallas kernels, mlp_part(): pl.pallas_call(mlp_kernel, out_shape=jax.ShapeDtypeStruct((n_rows, n_cols...  34.1 us
    all_gather x2, waiting for transfers between devices, local(): lax.all_gather(mine, 'lat', axis=0)  21.8 us
  transfers between devices with their start and end apart: 3, of which 1 were waited for; matrix products, arithmetic and copies ran while one was open for 0% of the time, Pallas kernels for 72%

profile of v2, /device:TPU:3, one launch (start us, length us, event | category | flops | bytes accessed | tf_op | source)
XLA Modules:
  0.0 222.3 jit_solution(1084049563914153999)
XLA Ops:
  7.2 0.0 copy-start.2
  7.2 0.0 all-gather.5.cloned.1.call-start
  7.2 2.9 %shard_map.159 = (bf16[128,2048]{1,0:T(8,128)(2,1)}, bf16[128,2048]{1,0:T(8,128)(2,1)}) custom-call(s32[2,2]{1,0:T(2,128)} %plan.5, bf16[1,2,64,4096]{3,2,1,0:T(8,128)(2,1)} %w_in.1, bf16[1,2,64,4096]{3,2,1,0:T(8,128)(2,1)} %w_out.1), custom_call_target="tpu_custom_call" | custom-call | tf_op jit(solution)/shard_map/pallas_call | solution.py:731
  10.1 0.0 all-gather.5.cloned.1.call-update
  10.1 0.0 all-gather.7.cloned.1.call-start
  10.2 0.7 all-gather.7.cloned.1.call-update
  10.9 0.0 copy-done.2
  10.9 1.3 collective-permute-start
  12.2 65.2 %shard_map.158 = (f32[7,90,1024]{2,1,0:T(8,128)}, bf16[7,96,1024]{2,1,0:T(8,128)(2,1)}, bf16[7,96,1024]{2,1,0:T(8,128)(2,1)}, bf16[2,4,7,96,128]{4,3,2,1,0:T(8,128)(2,1)}) custom-call(s32[2,2]{1,0:T(2,128)} %plan.5, s32[3]{0:T(128)} %cutoff.3, s32[2]{0:T(128)} %lmax.3, s32[2]{0:T(128)} %mmax.3, bf16[7,90,1024]{2,1,0:T(8,128)(2,1)} %bitcast.9, ...), custom_call_target="tpu_custom_call" | custom-call | flops 49999998976 | bytes 10000000 | tf_op jit(solution)/shard_map/pallas_call | solution.py:557
  77.5 21.8 %all-gather.5.cloned.1.call-done = bf16[2048,2048]{1,0:T(8,128)(2,1)} async-done(((bf16[128,2048]{1,0:T(8,128)(2,1)}), bf16[2048,2048]{1,0:T(8,128)(2,1)}) %all-gather.5.cloned.1.call-update) | async-done | bytes 8388624 | tf_op jit(solution)/shard_map/all_gather | solution.py:748
  99.3 17.1 %shard_map.160.refs_1_ = bf16[7,90,1024]{2,1,0:T(8,128)(2,1)} custom-call(f32[7,90,1024]{2,1,0:T(8,128)} %get-tuple-element.11.v_hbm, bf16[7,96,1024]{2,1,0:T(8,128)(2,1)} %get-tuple-element.12.own_hbm, bf16[7,96,1024]{2,1,0:T(8,128)(2,1)} %get-tuple-element.13.sib_hbm, bf16[16,128,2048]{2,1,0:T(8,128)(2,1)} %bitcast.8), custom_call_target="tpu_custom_call" | custom-call | flops 10000000000 | bytes 10000000 | tf_op jit(solution)/shard_map/pallas_call | solution.py:690
  116.4 0.0 collective-permute-done.refs_2_
  116.4 0.0 copy-start.3
  116.4 0.6 copy-done.3
  117.0 78.1 %shard_map.161 = (f32[7,90,1024]{2,1,0:T(8,128)}, bf16[7,96,1024]{2,1,0:T(8,128)(2,1)}, bf16[7,96,1024]{2,1,0:T(8,128)(2,1)}) custom-call(s32[2,2]{1,0:T(2,128)} %plan.5, s32[3]{0:T(128)} %cutoff.3, s32[2]{0:T(128)} %lmax.3, s32[2]{0:T(128)} %mmax.3, bf16[7,90,1024]{2,1,0:T(8,128)(2,1)} %refs_0_.1, bf16[7,90,1024]{2,1,0:T(8,128)(2,1)} %shard_map.160.refs_1_, ...), custom_call_target="tpu_custom_call" | custom-call | flops 49999998976 | bytes 10000000 | tf_op jit(solution)/shard_map/pallas_call | solution.py:557
  195.1 0.0 all-gather.7.cloned.1.call-done
  195.1 0.0 copy-start
  195.1 17.0 %shard_map.162 = bf16[7,90,1024]{2,1,0:T(8,128)(2,1)} custom-call(f32[7,90,1024]{2,1,0:T(8,128)} %get-tuple-element.16.v_hbm, bf16[7,96,1024]{2,1,0:T(8,128)(2,1)} %get-tuple-element.17.own_hbm, bf16[7,96,1024]{2,1,0:T(8,128)(2,1)} %get-tuple-element.18.sib_hbm, bf16[16,128,2048]{2,1,0:T(8,128)(2,1)} %bitcast.7), custom_call_target="tpu_custom_call" | custom-call | flops 10000000000 | bytes 10000000 | tf_op jit(solution)/shard_map/pallas_call | solution.py:690
  212.2 0.0 copy-done
  212.2 0.0 copy-start.1
  212.2 1.1 copy.19
  213.3 0.7 copy-done.1
  214.0 1.1 copy.20
Async XLA Ops:
  7.2 3.7 %copy-start.2 = (f32[1,2,2,1024]{3,2,1,0:T(2,128)S(1)}, f32[1,2,2,1024]{3,2,1,0:T(2,128)}, u32[]{:S(2)}) copy-start(f32[1,2,2,1024]{3,2,1,0:T(2,128)} %refs_5_.2) | copy-start | bytes 49156
  7.2 92.1 %all-gather.5.cloned.1.call-start = ((), (), s32[]{:S(2)}) async-start(), calls=%async_computation | async-start | bytes 8912896 | tf_op jit(solution)/shard_map/all_gather | solution.py:748
  10.1 185.0 %all-gather.7.cloned.1.call-start = ((), (), s32[]{:S(2)}) async-start(), calls=%async_computation.1 | async-start | bytes 8912896 | tf_op jit(solution)/shard_map/all_gather | solution.py:748
  10.9 105.5 %collective-permute-start = (f32[1,2,2,1024]{3,2,1,0:T(2,128)S(1)}, f32[1,2,2,1024]{3,2,1,0:T(2,128)S(1)}, u32[]{:S(2)}, u32[]{:S(2)}) collective-permute-start(f32[1,2,2,1024]{3,2,1,0:T(2,128)S(1)} %copy-done.2), channel_id=1, source_target_pairs={{64,0},{65,1},{66,2},{67,3},{68,4},{69,5},{70,6},{71,7},{72,8},{73... | collective-permute-start | bytes 49160 | tf_op jit(solution)/shard_map/ppermute | solution.py:26
  116.4 0.6 copy-start.3
  195.1 17.1 %copy-start = (bf16[7,90,1024]{2,1,0:T(8,128)(2,1)S(1)}, bf16[7,90,1024]{2,1,0:T(8,128)(2,1)}, u32[]{:S(2)}) copy-start(bf16[7,90,1024]{2,1,0:T(8,128)(2,1)} %shard_map.160.refs_1_) | copy-start | bytes 3870724
  212.2 1.8 copy-start.1
Sparse Core Ops, SparseCore 0:
  10.7 88.4 all-gather.4
  102.0 90.2 all-gather.6

commit v3 on v2

--- a/solution.py
+++ b/solution.py
@@ -99,7 +99,7 @@
     (
         tok, prior, norm, ahead, x_all, spec, y_all, y_f32, f_f32, back, z_all, o_all, r_all, vbuf, nbuf, leg, legt,
         a_send, a_recv, e_send, f_recv, t_send, t_recv, b_send, b_recv, c_send, c_recv, d_send, d_recv, n_send, n_recv, loc, row_in, next_sem,
-        stat, stat_all, raw_in, stat_send, stat_recv, raw_send, raw_recv,
+        stat, stat_in, stat_sem,
     ) = refs
     section, lat, lon = (lax.axis_index(a) for a in ("section", "lat", "lon"))
     n_lat = spec.shape[1]
@@ -198,25 +198,16 @@
             src_ref=ahead.at[h, peer, j], dst_ref=x_next.at[h, slot, j], send_sem=e_send.at[h, d, j],
             recv_sem=f_recv.at[h, d, j], device_id={"lon": peer}, device_id_type=MESH)
 
-    chip = lon // 2
-    far = pl.ds(pl.multiple_of((1 - chip) * 2 * part, part), 2 * part)
-
-    def copy_t(j):
-        return pltpu.make_async_remote_copy(
-            src_ref=prior.at[j, :, far], dst_ref=tok.at[j, :, far], send_sem=t_send.at[j], recv_sem=t_recv.at[j],
+    def copy_t(d):
+        quarter = pl.ds(pl.multiple_of(lon_peer(lon, d) * part, part), part)
+        return pltpu.make_async_remote_copy(
+            src_ref=prior.at[:, :, quarter], dst_ref=tok.at[:, :, quarter], send_sem=t_send.at[d], recv_sem=t_recv.at[d],
             device_id={"section": 1 - section}, device_id_type=MESH)
 
-    def copy_stat(d, sending):
-        peer = lon_peer(lon, d)
-        slot = lon if sending else peer
-        return pltpu.make_async_remote_copy(
-            src_ref=stat, dst_ref=stat_all.at[slot], send_sem=stat_send.at[d], recv_sem=stat_recv.at[d],
-            device_id={"section": 1 - section, "lon": peer}, device_id_type=MESH)
-
-    def copy_raw(h):
-        return pltpu.make_async_remote_copy(
-            src_ref=x_all.at[h, sibling], dst_ref=raw_in.at[h], send_sem=raw_send.at[h], recv_sem=raw_recv.at[h],
-            device_id={"lon": sibling}, device_id_type=MESH)
+    def copy_stat():
+        return pltpu.make_async_remote_copy(
+            src_ref=stat, dst_ref=stat_in, send_sem=stat_sem.at[0], recv_sem=stat_sem.at[1],
+            device_id={"section": 1 - section}, device_id_type=MESH)
 
     def split_into(dst, j, out):
         for q in range(4):
@@ -254,7 +245,7 @@
                 out = center * scale * next_gain
                 for q in range(4):
                     at = slice(q * part, (q + 1) * part)
-                    mixed = jnp.where(chip == q // 2, raw[:, at], out[:, at]).astype(BF16)
+                    mixed = jnp.where(lon == q, raw[:, at], out[:, at]).astype(BF16)
                     for h in (0, 1):
                         ahead[h, q, j, 0:n_cols, :] = mixed[:, h * half : (h + 1) * half]
                 for d in range(4):
@@ -267,10 +258,10 @@
                     copy_e(1, j, d).start()
 
             over_rows(norm_ahead)
-            for d in (0, 1):
-                copy_stat(d, True).start()
+            copy_stat().start()
             over_rows(norm_ahead_rest)
-            over_rows(lambda j: copy_t(j).start())
+            for d in (1, 2, 3):
+                copy_t(d).start()
     else:
         over_rows(first_norm)
         over_rows(first_norm_rest)
@@ -321,12 +312,12 @@
         if not handing:
             return x_all[h, :, j].reshape(4 * LON_PAD, half)
         shift, gain = of_lon(embed, h), of_lon(gain_one, h)
+        own = x_all[h, lon, j].astype(F32)
+        own = (own + shift - stat_in[:, 2 * j : 2 * j + 1]) * stat_in[:, 2 * j + 1 : 2 * j + 2] * gain
         rows_of = []
         for q in range(4):
-            raw = x_all[h, q, j].astype(F32)
-            out = (raw + shift - stat_all[q, :, 2 * j : 2 * j + 1]) * stat_all[q, :, 2 * j + 1 : 2 * j + 2] * gain
-            is_raw = jnp.logical_and(section > 0, chip == q // 2)
-            rows_of.append(jnp.where(is_raw, out, raw).astype(BF16))
+            is_raw = jnp.logical_and(section > 0, lon == q)
+            rows_of.append(jnp.where(is_raw, own, x_all[h, q, j].astype(F32)).astype(BF16))
         return jnp.concatenate(rows_of, axis=0)
 
     def zonal(h, first, count):
@@ -357,17 +348,10 @@
 
                 @pl.when(jnp.logical_not(first_section))
                 def _():
-                    for d in (0, 1):
-                        copy_stat(d, False).wait_recv()
+                    copy_stat().wait_recv()
 
         for first, count in ROWS:
             zonal(h, first, count)
-        if handing:
-
-            @pl.when(jnp.logical_not(first_section))
-            def _(h=h):
-                copy_raw(h).start()
-
         over_lat(lambda d, h=h: moved(spec, y_all, b_send, b_recv, True, h, d).start())
 
     rows = n_rows * MODE_PAD
@@ -453,16 +437,13 @@
 
         @pl.when(jnp.logical_not(first_section))
         def _():
-            for h in (0, 1):
-                copy_raw(h).wait_recv()
+            for d in (1, 2, 3):
+                copy_t(d).wait_recv()
 
             def assemble(j):
-                copy_t(j).wait_recv()
                 for h in (0, 1):
                     mine = pl.ds(pl.multiple_of(lon * part + h * half, half), half)
-                    other = pl.ds(pl.multiple_of(sibling * part + h * half, half), half)
                     tok[j, :, mine] = x_all[h, lon, j, 0:n_cols, :]
-                    tok[j, :, other] = raw_in[h, j, 0:n_cols, :]
 
             over_rows(assemble)
 
@@ -509,18 +490,13 @@
             for h in (0, 1):
                 for d in range(4):
                     copy_e(h, j, d).wait_send()
-            copy_t(j).wait_send()
 
         @pl.when(first_section)
         def _():
             over_rows(finish_handing)
-            for d in (0, 1):
-                copy_stat(d, True).wait_send()
-
-        @pl.when(jnp.logical_not(first_section))
-        def _():
-            for h in (0, 1):
-                copy_raw(h).wait_send()
+            copy_stat().wait_send()
+            for d in (1, 2, 3):
+                copy_t(d).wait_send()
     else:
 
         def finish_next(j):
@@ -573,16 +549,15 @@
             pltpu.VMEM(leg.shape[1:], BF16),
             pltpu.VMEM(legt.shape[1:], BF16),
             dma((2, 4, n_rows)), dma((2, 4, n_rows)), dma((2, 4, n_rows)), dma((2, 4, n_rows)),
-            dma((n_rows,)), dma((n_rows,)),
+            dma((4,)), dma((4,)),
             dma((2, n_lat)), dma((2, n_lat)),
             dma((2, n_lat)), dma((2, n_lat)),
             dma((2, 4, n_rows)), dma((2, 4, n_rows)),
             dma((n_rows,)), dma((n_rows,)),
             dma((2 + 2 * n_rows,)), dma((2, n_rows)), dma((2,)),
             pltpu.VMEM((LON_PAD, 128), F32),
-            pltpu.VMEM((4, LON_PAD, 128), F32),
-            pltpu.VMEM((2, n_rows, LON_PAD, half), BF16) if tick else small,
-            dma((2,)), dma((2,)), dma((2,)), dma((2,)),
+            pltpu.VMEM((LON_PAD, 128), F32),
+            dma((2,)),
         ],
         compiler_params=pltpu.CompilerParams(
             collective_id=2 * tick, has_side_effects=True, vmem_limit_bytes=VMEM),
@@ -709,14 +684,13 @@
     )(v, own, sib, weights)
 
 
-def pick_kernel(plan, w_in, w_out, first, second, sem):
+def pick_kernel(tick, plan, w_in, w_out, out, sem):
     section = lax.axis_index("section")
     core = lax.rem(lax.axis_index("lon"), 2)
     shard, ff = w_in.shape[2], w_in.shape[3] // 2
     columns = pl.ds(pl.multiple_of(core * ff, ff), ff)
     copies = [
-        pltpu.make_async_copy(ref.at[0, plan[tick, section], :, columns], out.at[pl.ds(k * shard, shard)], sem.at[tick, k])
-        for tick, out in enumerate((first, second))
+        pltpu.make_async_copy(ref.at[0, plan[tick, section], :, columns], out.at[pl.ds(k * shard, shard)], sem.at[k])
         for k, ref in enumerate((w_in, w_out))
     ]
     for copy in copies:
@@ -725,15 +699,15 @@
         copy.wait()
 
 
-def own_weights(plan, w_in, w_out):
+def own_weights(tick, plan, w_in, w_out):
     anys = pl.BlockSpec(memory_space=pltpu.HBM)
     out = jax.ShapeDtypeStruct((2 * w_in.shape[2], w_in.shape[3] // 2), BF16)
     return pl.pallas_call(
-        pick_kernel,
-        out_shape=(out, out),
+        functools.partial(pick_kernel, tick),
+        out_shape=out,
         in_specs=[pl.BlockSpec(memory_space=pltpu.SMEM), anys, anys],
-        out_specs=(pl.BlockSpec(memory_space=pltpu.VMEM),) * 2,
-        scratch_shapes=[pltpu.SemaphoreType.DMA((2, 2))],
+        out_specs=pl.BlockSpec(memory_space=pltpu.VMEM),
+        scratch_shapes=[pltpu.SemaphoreType.DMA((2,))],
         compiler_params=pltpu.CompilerParams(vmem_limit_bytes=VMEM),
     )(plan, w_in, w_out)
 
@@ -745,7 +719,7 @@
     n_rows, n_cols, width = fresh.shape
     n_degrees = filters.shape[3]
     tables = [jnp.asarray(t) for t in spectral_tables(n_lat, n_lon, n_rows, n_cols, n_degrees)]
-    weights = [lax.all_gather(mine, "lat", axis=0) for mine in own_weights(plan, w_in, w_out)]
+    weights = [lax.all_gather(own_weights(tick, plan, w_in, w_out), "lat", axis=0) for tick in (0, 1)]
     other_gains = passed_along(norm_gains, "section", -1)
 
     def spectral(tick, tokens, *more):

time: 227 us -> 215 us (0.947); the launches traced: 222 us -> 215 us
  waiting for transfers between devices: 22.5 us -> 18.6 us
  Pallas kernels: 180 us -> 177 us
    pallas_call x2, Pallas kernels: 143 us -> 138 us  [spectral_part(): pl.pallas_call(functools.partial(spec_kernel, tick, n_section), out_shape...]
    all_gather x2, waiting for transfers between devices: 21.8 us -> 18.6 us  [local(): lax.all_gather(own_weights(tick, plan, w_in, w_out), 'lat', axis=0)]
    pallas_call x1 -> x2, Pallas kernels: 2.89 us -> 5.08 us  [own_weights(): pl.pallas_call(functools.partial(pick_kernel, tick), out_shape=out, in_sp...]
  transfers between devices with their start and end apart: 3 -> 3, of which waited for: 1 -> 1; matrix products, arithmetic and copies ran while one was open for 0% -> 0% of each run, Pallas kernels for 72% -> 73%
where the time goes in v3:
time: 215 us
  Pallas kernels  177 us (82%)
  waiting for transfers between devices  18.6 us (9%)
  between operations  14.2 us (7%)
  local copies, waits for them, and re-layouts  3.52 us (2%)
    pallas_call x2, Pallas kernels, spectral_part(): pl.pallas_call(functools.partial(spec_kernel, tick, n_section), out_shape...  138 us
    pallas_call x2, Pallas kernels, mlp_part(): pl.pallas_call(mlp_kernel, out_shape=jax.ShapeDtypeStruct((n_rows, n_cols...  34.1 us
    all_gather x2, waiting for transfers between devices, local(): lax.all_gather(own_weights(tick, plan, w_in, w_out), 'lat', axis=0)  18.6 us
    pallas_call x2, Pallas kernels, own_weights(): pl.pallas_call(functools.partial(pick_kernel, tick), out_shape=out, in_sp...  5.08 us
  transfers between devices with their start and end apart: 3, of which 1 were waited for; matrix products, arithmetic and copies ran while one was open for 0% of the time, Pallas kernels for 73%

profile of v3, /device:TPU:3, one launch (start us, length us, event | category | flops | bytes accessed | tf_op | source)
XLA Modules:
  0.0 214.7 jit_solution(9545492657181739590)
XLA Ops:
  7.2 0.0 all-gather.5.cloned.1.call-start
  7.2 2.5 %shard_map.159 = bf16[128,2048]{1,0:T(8,128)(2,1)} custom-call(s32[2,2]{1,0:T(2,128)} %plan.7, bf16[1,2,64,4096]{3,2,1,0:T(8,128)(2,1)} %w_in.3, bf16[1,2,64,4096]{3,2,1,0:T(8,128)(2,1)} %w_out.3), custom_call_target="tpu_custom_call" | custom-call | tf_op jit(solution)/shard_map/pallas_call | solution.py:705
  9.8 0.0 all-gather.5.cloned.1.call-update
  9.8 0.0 copy-start.2
  9.8 0.0 all-gather.7.cloned.1.call-start
  9.8 2.5 %shard_map.162 = bf16[128,2048]{1,0:T(8,128)(2,1)} custom-call(s32[2,2]{1,0:T(2,128)} %plan.7, bf16[1,2,64,4096]{3,2,1,0:T(8,128)(2,1)} %w_in.3, bf16[1,2,64,4096]{3,2,1,0:T(8,128)(2,1)} %w_out.3), custom_call_target="tpu_custom_call" | custom-call | tf_op jit(solution)/shard_map/pallas_call | solution.py:705
  12.4 0.0 all-gather.7.cloned.1.call-update
  12.4 0.0 copy-done.2
  12.4 1.3 collective-permute-start
  13.8 63.8 %shard_map.158 = (f32[7,90,1024]{2,1,0:T(8,128)}, bf16[7,96,1024]{2,1,0:T(8,128)(2,1)}, bf16[7,96,1024]{2,1,0:T(8,128)(2,1)}, bf16[2,4,7,96,128]{4,3,2,1,0:T(8,128)(2,1)}) custom-call(s32[2,2]{1,0:T(2,128)} %plan.7, s32[3]{0:T(128)} %cutoff.3, s32[2]{0:T(128)} %lmax.3, s32[2]{0:T(128)} %mmax.3, bf16[7,90,1024]{2,1,0:T(8,128)(2,1)} %bitcast.9, ...), custom_call_target="tpu_custom_call" | custom-call | flops 49999998976 | bytes 10000000 | tf_op jit(solution)/shard_map/pallas_call | solution.py:533
  77.6 18.5 %all-gather.5.cloned.1.call-done = bf16[2048,2048]{1,0:T(8,128)(2,1)} async-done(((bf16[128,2048]{1,0:T(8,128)(2,1)}), bf16[2048,2048]{1,0:T(8,128)(2,1)}) %all-gather.5.cloned.1.call-update) | async-done | bytes 8388624 | tf_op jit(solution)/shard_map/all_gather | solution.py:722
  96.1 17.1 %shard_map.160.refs_1_ = bf16[7,90,1024]{2,1,0:T(8,128)(2,1)} custom-call(f32[7,90,1024]{2,1,0:T(8,128)} %get-tuple-element.9.v_hbm, bf16[7,96,1024]{2,1,0:T(8,128)(2,1)} %get-tuple-element.10.own_hbm, bf16[7,96,1024]{2,1,0:T(8,128)(2,1)} %get-tuple-element.11.sib_hbm, bf16[16,128,2048]{2,1,0:T(8,128)(2,1)} %bitcast.8), custom_call_target="tpu_custom_call" | custom-call | flops 10000000000 | bytes 10000000 | tf_op jit(solution)/shard_map/pallas_call | solution.py:665
  113.2 0.0 collective-permute-done.refs_2_
  113.2 0.0 copy-start.3
  113.3 0.6 copy-done.3
  113.9 74.0 %shard_map.161 = (f32[7,90,1024]{2,1,0:T(8,128)}, bf16[7,96,1024]{2,1,0:T(8,128)(2,1)}, bf16[7,96,1024]{2,1,0:T(8,128)(2,1)}) custom-call(s32[2,2]{1,0:T(2,128)} %plan.7, s32[3]{0:T(128)} %cutoff.3, s32[2]{0:T(128)} %lmax.3, s32[2]{0:T(128)} %mmax.3, bf16[7,90,1024]{2,1,0:T(8,128)(2,1)} %refs_0_.1, bf16[7,90,1024]{2,1,0:T(8,128)(2,1)} %shard_map.160.refs_1_, ...), custom_call_target="tpu_custom_call" | custom-call | flops 49999998976 | bytes 10000000 | tf_op jit(solution)/shard_map/pallas_call | solution.py:533
  187.8 0.0 all-gather.7.cloned.1.call-done
  187.8 0.0 copy-start
  187.9 17.0 %shard_map.163 = bf16[7,90,1024]{2,1,0:T(8,128)(2,1)} custom-call(f32[7,90,1024]{2,1,0:T(8,128)} %get-tuple-element.13.v_hbm, bf16[7,96,1024]{2,1,0:T(8,128)(2,1)} %get-tuple-element.14.own_hbm, bf16[7,96,1024]{2,1,0:T(8,128)(2,1)} %get-tuple-element.15.sib_hbm, bf16[16,128,2048]{2,1,0:T(8,128)(2,1)} %bitcast.7), custom_call_target="tpu_custom_call" | custom-call | flops 10000000000 | bytes 10000000 | tf_op jit(solution)/shard_map/pallas_call | solution.py:665
  204.9 0.0 copy-done
  204.9 0.0 copy-start.1
  204.9 1.1 copy.19
  206.0 0.7 copy-done.1
  206.8 1.1 copy.20
Async XLA Ops:
  7.2 89.0 %all-gather.5.cloned.1.call-start = ((), (), s32[]{:S(2)}) async-start(), calls=%async_computation | async-start | bytes 8912896 | tf_op jit(solution)/shard_map/all_gather | solution.py:722
  9.8 2.6 %copy-start.2 = (f32[1,2,2,1024]{3,2,1,0:T(2,128)S(1)}, f32[1,2,2,1024]{3,2,1,0:T(2,128)}, u32[]{:S(2)}) copy-start(f32[1,2,2,1024]{3,2,1,0:T(2,128)} %refs_5_.2) | copy-start | bytes 49156
  9.8 178.0 %all-gather.7.cloned.1.call-start = ((), (), s32[]{:S(2)}) async-start(), calls=%async_computation.1 | async-start | bytes 8912896 | tf_op jit(solution)/shard_map/all_gather | solution.py:722
  12.4 100.8 %collective-permute-start = (f32[1,2,2,1024]{3,2,1,0:T(2,128)S(1)}, f32[1,2,2,1024]{3,2,1,0:T(2,128)S(1)}, u32[]{:S(2)}, u32[]{:S(2)}) collective-permute-start(f32[1,2,2,1024]{3,2,1,0:T(2,128)S(1)} %copy-done.2), channel_id=1, source_target_pairs={{64,0},{65,1},{66,2},{67,3},{68,4},{69,5},{70,6},{71,7},{72,8},{73... | collective-permute-start | bytes 49160 | tf_op jit(solution)/shard_map/ppermute | solution.py:26
  113.2 0.6 copy-start.3
  187.8 17.1 %copy-start = (bf16[7,90,1024]{2,1,0:T(8,128)(2,1)S(1)}, bf16[7,90,1024]{2,1,0:T(8,128)(2,1)}, u32[]{:S(2)}) copy-start(bf16[7,90,1024]{2,1,0:T(8,128)(2,1)} %shard_map.160.refs_1_) | copy-start | bytes 3870724
  204.9 1.8 copy-start.1
Sparse Core Ops, SparseCore 0:
  10.7 85.3 all-gather.4
  98.8 88.4 all-gather.6

commit v4 on v3

--- a/solution.py
+++ b/solution.py
@@ -352,7 +352,11 @@
 
         for first, count in ROWS:
             zonal(h, first, count)
-        over_lat(lambda d, h=h: moved(spec, y_all, b_send, b_recv, True, h, d).start())
+        if handing:
+            over_lat(lambda d, h=h: moved(spec, y_all, b_send, b_recv, True, h, d).start())
+    if not handing:
+        for h in (0, 1):
+            over_lat(lambda d, h=h: moved(spec, y_all, b_send, b_recv, True, h, d).start())
 
     rows = n_rows * MODE_PAD
     n_lines = n_lat * n_rows

time: 215 us -> 214 us (level)
  waiting for transfers between devices: 18.6 us -> 7.73 us
  Pallas kernels: 177 us -> 187 us
    all_gather x2, waiting for transfers between devices: 18.6 us -> 7.69 us  [local(): lax.all_gather(own_weights(tick, plan, w_in, w_out), 'lat', axis=0)]
    pallas_call x2, Pallas kernels: 138 us -> 148 us  [spectral_part(): pl.pallas_call(functools.partial(spec_kernel, tick, n_section), out_shape...]
  transfers between devices with their start and end apart: 3 -> 3, of which waited for: 1 -> 2; matrix products, arithmetic and copies ran while one was open for 0% -> 0% of each run, Pallas kernels for 73% -> 78%
where the time goes in v4:
time: 214 us
  Pallas kernels  187 us (87%)
  between operations  14.1 us (7%)
  waiting for transfers between devices  7.73 us (4%)
  local copies, waits for them, and re-layouts  3.52 us (2%)
    pallas_call x2, Pallas kernels, spectral_part(): pl.pallas_call(functools.partial(spec_kernel, tick, n_section), out_shape...  148 us
    pallas_call x2, Pallas kernels, mlp_part(): pl.pallas_call(mlp_kernel, out_shape=jax.ShapeDtypeStruct((n_rows, n_cols...  34 us
    all_gather x2, waiting for transfers between devices, local(): lax.all_gather(own_weights(tick, plan, w_in, w_out), 'lat', axis=0)  7.69 us
    pallas_call x2, Pallas kernels, own_weights(): pl.pallas_call(functools.partial(pick_kernel, tick), out_shape=out, in_sp...  5.08 us
  transfers between devices with their start and end apart: 3, of which 2 were waited for; matrix products, arithmetic and copies ran while one was open for 0% of the time, Pallas kernels for 78%

profile of v4, /device:TPU:3, one launch (start us, length us, event | category | flops | bytes accessed | tf_op | source)
XLA Modules:
  0.0 213.9 jit_solution(5857486039496053452)
XLA Ops:
  7.2 0.0 all-gather.5.cloned.1.call-start
  7.2 2.5 %shard_map.159 = bf16[128,2048]{1,0:T(8,128)(2,1)} custom-call(s32[2,2]{1,0:T(2,128)} %plan.7, bf16[1,2,64,4096]{3,2,1,0:T(8,128)(2,1)} %w_in.3, bf16[1,2,64,4096]{3,2,1,0:T(8,128)(2,1)} %w_out.3), custom_call_target="tpu_custom_call" | custom-call | tf_op jit(solution)/shard_map/pallas_call | solution.py:709
  9.8 0.0 all-gather.5.cloned.1.call-update
  9.8 0.0 copy-start.2
  9.8 0.0 all-gather.7.cloned.1.call-start
  9.8 2.5 %shard_map.162 = bf16[128,2048]{1,0:T(8,128)(2,1)} custom-call(s32[2,2]{1,0:T(2,128)} %plan.7, bf16[1,2,64,4096]{3,2,1,0:T(8,128)(2,1)} %w_in.3, bf16[1,2,64,4096]{3,2,1,0:T(8,128)(2,1)} %w_out.3), custom_call_target="tpu_custom_call" | custom-call | tf_op jit(solution)/shard_map/pallas_call | solution.py:709
  12.4 0.0 all-gather.7.cloned.1.call-update
  12.4 0.0 copy-done.2
  12.4 1.3 collective-permute-start
  13.8 75.7 %shard_map.158 = (f32[7,90,1024]{2,1,0:T(8,128)}, bf16[7,96,1024]{2,1,0:T(8,128)(2,1)}, bf16[7,96,1024]{2,1,0:T(8,128)(2,1)}, bf16[2,4,7,96,128]{4,3,2,1,0:T(8,128)(2,1)}) custom-call(s32[2,2]{1,0:T(2,128)} %plan.7, s32[3]{0:T(128)} %cutoff.3, s32[2]{0:T(128)} %lmax.3, s32[2]{0:T(128)} %mmax.3, bf16[7,90,1024]{2,1,0:T(8,128)(2,1)} %bitcast.9, ...), custom_call_target="tpu_custom_call" | custom-call | flops 49999998976 | bytes 10000000 | tf_op jit(solution)/shard_map/pallas_call | solution.py:537
  89.5 7.2 %all-gather.5.cloned.1.call-done = bf16[2048,2048]{1,0:T(8,128)(2,1)} async-done(((bf16[128,2048]{1,0:T(8,128)(2,1)}), bf16[2048,2048]{1,0:T(8,128)(2,1)}) %all-gather.5.cloned.1.call-update) | async-done | bytes 8388624 | tf_op jit(solution)/shard_map/all_gather | solution.py:726
  96.7 17.1 %shard_map.160.refs_1_ = bf16[7,90,1024]{2,1,0:T(8,128)(2,1)} custom-call(f32[7,90,1024]{2,1,0:T(8,128)} %get-tuple-element.9.v_hbm, bf16[7,96,1024]{2,1,0:T(8,128)(2,1)} %get-tuple-element.10.own_hbm, bf16[7,96,1024]{2,1,0:T(8,128)(2,1)} %get-tuple-element.11.sib_hbm, bf16[16,128,2048]{2,1,0:T(8,128)(2,1)} %bitcast.8), custom_call_target="tpu_custom_call" | custom-call | flops 10000000000 | bytes 10000000 | tf_op jit(solution)/shard_map/pallas_call | solution.py:669
  113.8 0.0 collective-permute-done.refs_2_
  113.8 0.0 copy-start.3
  113.9 0.6 copy-done.3
  114.5 72.3 %shard_map.161 = (f32[7,90,1024]{2,1,0:T(8,128)}, bf16[7,96,1024]{2,1,0:T(8,128)(2,1)}, bf16[7,96,1024]{2,1,0:T(8,128)(2,1)}) custom-call(s32[2,2]{1,0:T(2,128)} %plan.7, s32[3]{0:T(128)} %cutoff.3, s32[2]{0:T(128)} %lmax.3, s32[2]{0:T(128)} %mmax.3, bf16[7,90,1024]{2,1,0:T(8,128)(2,1)} %refs_0_.1, bf16[7,90,1024]{2,1,0:T(8,128)(2,1)} %shard_map.160.refs_1_, ...), custom_call_target="tpu_custom_call" | custom-call | flops 49999998976 | bytes 10000000 | tf_op jit(solution)/shard_map/pallas_call | solution.py:537
  186.7 0.5 all-gather.7.cloned.1.call-done
  187.2 0.0 copy-start
  187.2 17.0 %shard_map.163 = bf16[7,90,1024]{2,1,0:T(8,128)(2,1)} custom-call(f32[7,90,1024]{2,1,0:T(8,128)} %get-tuple-element.13.v_hbm, bf16[7,96,1024]{2,1,0:T(8,128)(2,1)} %get-tuple-element.14.own_hbm, bf16[7,96,1024]{2,1,0:T(8,128)(2,1)} %get-tuple-element.15.sib_hbm, bf16[16,128,2048]{2,1,0:T(8,128)(2,1)} %bitcast.7), custom_call_target="tpu_custom_call" | custom-call | flops 10000000000 | bytes 10000000 | tf_op jit(solution)/shard_map/pallas_call | solution.py:669
  204.1 0.0 copy-done
  204.2 0.0 copy-start.1
  204.2 1.1 copy.19
  205.2 0.7 copy-done.1
  206.0 1.1 copy.20
Async XLA Ops:
  7.2 89.6 %all-gather.5.cloned.1.call-start = ((), (), s32[]{:S(2)}) async-start(), calls=%async_computation | async-start | bytes 8912896 | tf_op jit(solution)/shard_map/all_gather | solution.py:726
  9.8 2.6 %copy-start.2 = (f32[1,2,2,1024]{3,2,1,0:T(2,128)S(1)}, f32[1,2,2,1024]{3,2,1,0:T(2,128)}, u32[]{:S(2)}) copy-start(f32[1,2,2,1024]{3,2,1,0:T(2,128)} %refs_5_.2) | copy-start | bytes 49156
  9.8 177.4 %all-gather.7.cloned.1.call-start = ((), (), s32[]{:S(2)}) async-start(), calls=%async_computation.1 | async-start | bytes 8912896 | tf_op jit(solution)/shard_map/all_gather | solution.py:726
  12.4 101.4 %collective-permute-start = (f32[1,2,2,1024]{3,2,1,0:T(2,128)S(1)}, f32[1,2,2,1024]{3,2,1,0:T(2,128)S(1)}, u32[]{:S(2)}, u32[]{:S(2)}) collective-permute-start(f32[1,2,2,1024]{3,2,1,0:T(2,128)S(1)} %copy-done.2), channel_id=1, source_target_pairs={{64,0},{65,1},{66,2},{67,3},{68,4},{69,5},{70,6},{71,7},{72,8},{73... | collective-permute-start | bytes 49160 | tf_op jit(solution)/shard_map/ppermute | solution.py:26
  113.8 0.6 copy-start.3
  187.2 17.0 %copy-start = (bf16[7,90,1024]{2,1,0:T(8,128)(2,1)S(1)}, bf16[7,90,1024]{2,1,0:T(8,128)(2,1)}, u32[]{:S(2)}) copy-start(bf16[7,90,1024]{2,1,0:T(8,128)(2,1)} %shard_map.160.refs_1_) | copy-start | bytes 3870724
  204.2 1.8 copy-start.1
Sparse Core Ops, SparseCore 0:
  10.7 85.9 all-gather.4
  99.4 87.6 all-gather.6
